TPU v7x, 32 devices: a whole 2x2x4 slice. The times are simulated.
32 devices in a mesh: tok: 16 (over z, y, x), head: 2 (over core).
Axes of the slice: x: 2, y: 2, z: 4, core: 2. Of those that a mesh axis runs over, the one named last changes fastest.
Arguments:
- tokens: bfloat16 [32768, 768], P(('tok', 'head')), may hold values from -6 to 6
- cotangent: bfloat16 [32768, 768], P(('tok', 'head')), may hold values from -6 to 6
- block_source: int32 [32, 4, 2], replicated, may hold values from 0 to 1, as said below
- mask_index: int32 [32, 256], replicated, may hold values from 0 to 1023, as said below
- mask_count: int32 [32], replicated, may hold values from 51 to 256
- w_query: bfloat16 [768, 768], P(None, 'head'), may hold values from -0.21875 to 0.21875
- w_key: bfloat16 [768, 768], P(None, 'head'), may hold values from -0.21875 to 0.21875
- w_value: bfloat16 [768, 768], P(None, 'head'), may hold values from -0.21875 to 0.21875
- w_output: bfloat16 [768, 768], P('head'), may hold values from -3 to 3
- mid_gain: float32 [768], replicated, may hold values from 0.25 to 1.75
- mid_shift: float32 [768], replicated, may hold values from -3 to 3
- w_inner: bfloat16 [768, 3072], P(None, 'head'), may hold values from -0.21875 to 0.21875
- bias_inner: float32 [3072], P('head'), may hold values from -3 to 3
- w_outer: bfloat16 [3072, 768], P('head'), may hold values from -0.109375 to 0.109375
- bias_outer: float32 [768], replicated, may hold values from -3 to 3
- end_gain: float32 [768], replicated, may hold values from 0.25 to 1.75
- end_shift: float32 [768], replicated, may hold values from -3 to 3
Outputs:
- out: bfloat16 [32768, 768], P(('tok', 'head'))
- grad_tokens: float32 [32768, 768], P(('tok', 'head'))
- grad_w_query: float32 [768, 768], P(None, 'head')
- grad_w_key: float32 [768, 768], P(None, 'head')
- grad_w_value: float32 [768, 768], P(None, 'head')
- grad_w_output: float32 [768, 768], P('head')
- grad_mid_gain: float32 [768], replicated
- grad_mid_shift: float32 [768], replicated
- grad_w_inner: float32 [768, 3072], P(None, 'head')
- grad_bias_inner: float32 [3072], P('head')
- grad_w_outer: float32 [3072, 768], P('head')
- grad_bias_outer: float32 [768], replicated
- grad_end_gain: float32 [768], replicated
- grad_end_shift: float32 [768], replicated
Inputs may be any that keep to these rules, and one draw needn't show every extreme that they name: Each pair block_source[s, g] is (0, 1) or (1, 0); in every sequence at least one group has (1, 0). `mask_index`: the entries of a row are distinct positions of its sequence; only the first mask_count entries of a row are read.
All inputs are finite; a program needn't handle non-finite values.
Results may differ from a plain program's by a relative error of at most 0.015.
Values may be sent and summed in bfloat16 or wider, within the bound.
No kernel may reach another device: no remote copies, remote signals or barrier semaphores. Data moves between devices by JAX's collectives and lax.ppermute only.
A program may use at most 192 MiB of HBM per device.

v0:
```python
import functools
import math

import jax
import jax.numpy as jnp
from jax import lax
from jax.experimental import pallas as pl
from jax.experimental.pallas import tpu as pltpu
from jax.sharding import PartitionSpec as P

HEADS = 12
HDIM = 64
GROUPS = 4
BLOCK = 512
PAIR_SEQS = 4
LANES = 128

NORM_EPS = 1e-05
LOG2E = 1.4426950408889634
BF16 = jnp.bfloat16
F32 = jnp.float32


def swap_bit(x, axis, bit):
    return lax.ppermute(x, axis, [(i, i ^ 1 << bit) for i in range(lax.axis_size(axis))])


def dot(a, b, dims=((1,), (0,))):
    return lax.dot_general(a, b, (dims, ((), ())), preferred_element_type=F32)


NT = ((1,), (1,))
TN = ((0,), (0,))


def head_lanes(first):
    lane = lax.broadcasted_iota(jnp.int32, (1, LANES), 1)
    return (lane < HDIM) if first else (lane >= HDIM)


def vmem(limit=56):
    return pltpu.CompilerParams(vmem_limit_bytes=limit * 1024 * 1024)


def whole(shape):
    return pl.BlockSpec(shape, lambda *_: (0,) * len(shape), pipeline_mode=pl.Buffered(1))


def hbm(*arrays):
    return [pltpu.with_memory_space_constraint(x, pltpu.HBM) for x in arrays]


def pick(own, w_own_ref, w_mate_ref):
    return jnp.where(own, w_own_ref[...], w_mate_ref[...])


def normalize(summed):
    center = summed - jnp.mean(summed, axis=-1, keepdims=True)
    rate = lax.rsqrt(jnp.mean(center * center, axis=-1, keepdims=True) + NORM_EPS)
    return center * rate, rate


def norm_back(grad, normed, rate, gain):
    scaled = grad * gain
    return rate * (
        scaled
        - jnp.mean(scaled, axis=-1, keepdims=True)
        - normed * jnp.mean(scaled * normed, axis=-1, keepdims=True)
    )


def gelu_parts(u):
    size = jnp.abs(u)
    bell = jnp.exp2(u * u * (-0.5 * LOG2E))
    t = 1.0 / (1.0 + (0.3275911 * 0.5**0.5) * size)
    poly = t * (
        0.5 * 0.254829592
        + t
        * (
            0.5 * -0.284496736
            + t * (0.5 * 1.421413741 + t * (0.5 * -1.453152027 + t * (0.5 * 1.061405429)))
        )
    )
    tail = poly * bell
    phi = jnp.where(u > 0, 1.0 - tail, tail)
    return u * phi, phi + u * (bell * 0.3989422804014327)


SLOTS = (slice(0, BLOCK), slice(BLOCK, 2 * BLOCK))


def attend_kernel(
    pairs, swap_ref, xa_ref, xb_ref, wq_ref, wk_ref, wv_ref, mq_ref, mk_ref, mv_ref, wo_ref, mo_ref,
    qkv_ref, lse_ref, ctx_t_ref, x_t_ref, mid_n_ref, rate_ref, ctx_all,
):
    step = pl.program_id(0)
    own = step < pairs // 2
    swap = swap_ref[...] > 0
    scale = LOG2E * HDIM**-0.5
    ones = jnp.ones((16, BLOCK), BF16)
    w = jnp.concatenate(
        [pick(own, wq_ref, mq_ref), pick(own, wk_ref, mk_ref), pick(own, wv_ref, mv_ref)], axis=1
    )
    for rows, x_ref in zip(SLOTS, (xa_ref, xb_ref)):
        qkv_ref[rows, :] = dot(x_ref[...], w).astype(BF16)
    keys = [qkv_ref[rows, LANES : 2 * LANES] for rows in SLOTS]
    values = [qkv_ref[rows, 2 * LANES :] for rows in SLOTS]
    units = []
    for i, rows in enumerate(SLOTS):
        q = qkv_ref[rows, :LANES]
        k = jnp.where(swap, keys[1 - i], keys[i])
        v_t = jnp.where(swap, values[1 - i], values[i]).T
        for n in (0, 1):
            q_n = jnp.where(head_lanes(n == 0), q, jnp.zeros_like(q))
            units.append((rows, n, v_t, dot(k, q_n, NT)))
    parts = []
    for rows, n, v_t, s in units:
        top = jnp.max(s, axis=0, keepdims=True)
        p = jnp.exp2((s - top) * scale).astype(BF16)
        v_n = jnp.concatenate([v_t[n * HDIM : (n + 1) * HDIM], ones], axis=0)
        acc = dot(v_n, p)
        total = acc[HDIM : HDIM + 1]
        parts.append(acc[:HDIM] / total)
        lse_ref[0, n : n + 1, rows] = top * scale + jnp.log2(total)
        if n == 1:
            ctx_t = jnp.concatenate(parts, axis=0)
            parts = []
            ctx_t_ref[:, rows] = ctx_t.astype(BF16)
            ctx_all[step, rows, :] = ctx_t.T.astype(BF16)

    cols = pl.ds(pl.multiple_of(step * LANES, LANES), LANES)
    for rows, x_ref in zip(SLOTS, (xa_ref, xb_ref)):
        x_t_ref[:, rows] = x_ref[:, cols].T

    @pl.when(step == pairs - 1)
    def _():
        for rows, x_ref in zip(SLOTS, (xa_ref, xb_ref)):
            total = x_ref[...].astype(F32)
            every = jnp.concatenate([ctx_all[p, rows, :] for p in range(pairs)], axis=1)
            cut = wo_ref.shape[0]
            total = total + dot(every[:, :cut], wo_ref[...]) + dot(every[:, cut:], mo_ref[...])
            normed, rate = normalize(total)
            mid_n_ref[rows, :] = normed
            rate_ref[rows, :] = rate


def attention(swap_lanes, blocks, own_w, mate_w, own_out, mate_out):
    width = blocks[0].shape[1]
    rows = 2 * BLOCK
    pairs = width // LANES
    per = own_w[0].shape[1] // LANES
    own_spec = pl.BlockSpec((width, LANES), lambda p: (0, jnp.minimum(p, per - 1)))
    mate_spec = pl.BlockSpec((width, LANES), lambda p: (0, jnp.maximum(p - per, 0)))
    return pl.pallas_call(
        functools.partial(attend_kernel, pairs),
        grid=(pairs,),
        in_specs=[pl.BlockSpec((1, LANES), lambda p: (0, p))]
        + [whole((BLOCK, width))] * 2
        + [own_spec] * 3
        + [mate_spec] * 3
        + [whole(own_out.shape)] * 2,
        out_specs=[
            pl.BlockSpec((rows, 3 * LANES), lambda p: (0, p)),
            pl.BlockSpec((1, 2, rows), lambda p: (p, 0, 0)),
            pl.BlockSpec((LANES, rows), lambda p: (p, 0)),
            pl.BlockSpec((LANES, rows), lambda p: (p, 0)),
            whole((rows, width)),
            whole((rows, 1)),
        ],
        out_shape=[
            pltpu.HBM((rows, 3 * width), BF16),
            jax.ShapeDtypeStruct((pairs, 2, rows), F32),
            pltpu.HBM((width, rows), BF16),
            pltpu.HBM((width, rows), BF16),
            pltpu.HBM((rows, width), F32),
            pltpu.HBM((rows, 1), F32),
        ],
        scratch_shapes=[pltpu.VMEM((pairs, rows, LANES), BF16)],
        compiler_params=vmem(28),
        cost_estimate=pl.CostEstimate(
            flops=2 * rows * width * width * 4 + 4 * pairs * 4 * BLOCK * BLOCK * 256,
            bytes_accessed=rows * width * 18 + width * width * 8,
            transcendentals=4 * pairs * BLOCK * BLOCK,
        ),
        name="attention_forward",
    )(swap_lanes, *blocks, *hbm(*own_w, *mate_w, own_out, mate_out))


def ffn_kernel(
    tiles, mid_n_ref, par_ref, wi_ref, mi_ref, bi_ref, mbi_ref, wd_ref, md_ref, ca_ref, cb_ref, wt_ref,
    act_t_ref, slope_ref, h1_t_ref, out_ref, ds2_ref, df_ref, vec_ref, gm_ref, h1_low, acc, act_m,
):
    step = pl.program_id(0)
    own = step < tiles // 2

    @pl.when(step == 0)
    def _():
        for rows in SLOTS:
            h1 = mid_n_ref[rows, :] * par_ref[0:1, :] + par_ref[1:2, :]
            low = h1.astype(BF16)
            h1_low[rows, :] = low
            h1_t_ref[:, rows] = low.T
            acc[rows, :] = h1 + par_ref[2:3, :]

    size = 256

    def tile(w_in, w_down, bias, act_ref):
        cuts = [slice(at, at + size) for at in range(0, 2 * BLOCK, size)]
        ready = [dot(h1_low[cuts[0], :], w_in)]
        for at, rows in enumerate(cuts):
            if at + 1 < len(cuts):
                ready.append(dot(h1_low[cuts[at + 1], :], w_in))
            value, slope = gelu_parts(ready[at] + bias)
            low = value.astype(BF16)
            slope_ref[rows, :] = slope.astype(BF16)
            act_ref[:, rows] = low.T
            acc[rows, :] += dot(low, w_down)

    @pl.when(own)
    def _():
        tile(wi_ref[...], wd_ref[...], bi_ref[...], act_t_ref)

    @pl.when(jnp.logical_and(step >= tiles // 2, step < tiles))
    def _():
        tile(mi_ref[...], md_ref[...], mbi_ref[...], act_m.at[step - tiles // 2])

    @pl.when(step >= tiles)
    def _():
        gm_ref[...] = dot(act_m[step - tiles], df_ref[...]).astype(BF16)

    @pl.when(step == tiles - 1)
    def _():
        gain = par_ref[3:4, :]
        sums = [0.0, 0.0, 0.0]
        for at in range(0, 2 * BLOCK, size):
            rows = slice(at, at + size)
            normed, rate = normalize(acc[rows, :])
            out_ref[rows, :] = (normed * gain + par_ref[4:5, :]).astype(BF16)
            cot_ref, first = (ca_ref, at) if at < BLOCK else (cb_ref, at - BLOCK)
            d_y = cot_ref[first : first + size, :].astype(F32) * wt_ref[rows, :]
            d_s2 = norm_back(d_y, normed, rate, gain)
            ds2_ref[rows, :] = d_s2
            df_ref[rows, :] = d_s2.astype(BF16)
            for n, term in enumerate((d_y, d_y * normed, d_s2)):
                sums[n] = sums[n] + jnp.sum(term, axis=0, keepdims=True)
        vec_ref[...] = jnp.concatenate(sums + [jnp.zeros((5, gain.shape[1]), F32)], axis=0)


TILE = 768
COLS = 384


def ffn(mid_n, params, own_in, mate_in, own_bias, mate_bias, own_down, mate_down, cot, weight):
    rows, width = mid_n.shape
    per = own_in.shape[1] // TILE
    tiles = 2 * per

    def own_at(j):
        return jnp.minimum(j, per - 1)

    def mate_at(j):
        return jnp.clip(j - per, 0, per - 1)

    hidden = 2 * own_in.shape[1]
    return pl.pallas_call(
        functools.partial(ffn_kernel, tiles),
        grid=(tiles + per,),
        in_specs=[
            whole((rows, width)),
            whole(params.shape),
            pl.BlockSpec((width, TILE), lambda j: (0, own_at(j))),
            pl.BlockSpec((width, TILE), lambda j: (0, mate_at(j))),
            pl.BlockSpec((1, TILE), lambda j: (0, own_at(j))),
            pl.BlockSpec((1, TILE), lambda j: (0, mate_at(j))),
            pl.BlockSpec((TILE, width), lambda j: (own_at(j), 0)),
            pl.BlockSpec((TILE, width), lambda j: (mate_at(j), 0)),
            whole((BLOCK, width)),
            whole((BLOCK, width)),
            whole((rows, 1)),
        ],
        out_specs=[
            pl.BlockSpec((TILE, rows), lambda j: (own_at(j), 0)),
            pl.BlockSpec((rows, TILE), lambda j: (0, jnp.minimum(j, tiles - 1))),
            whole((width, rows)),
            whole((rows, width)),
            whole((rows, width)),
            whole((rows, width)),
            whole((8, width)),
            pl.BlockSpec((TILE, width), lambda j: (jnp.maximum(j - tiles, 0), 0)),
        ],
        out_shape=[
            jax.ShapeDtypeStruct((hidden // 2, rows), BF16),
            pltpu.HBM((rows, hidden), BF16),
            jax.ShapeDtypeStruct((width, rows), BF16),
            jax.ShapeDtypeStruct((rows, width), BF16),
            jax.ShapeDtypeStruct((rows, width), F32),
            jax.ShapeDtypeStruct((rows, width), BF16),
            jax.ShapeDtypeStruct((8, width), F32),
            jax.ShapeDtypeStruct((hidden // 2, width), BF16),
        ],
        scratch_shapes=[
            pltpu.VMEM((rows, width), BF16),
            pltpu.VMEM((rows, width), F32),
            pltpu.VMEM((per, TILE, rows), BF16),
        ],
        compiler_params=vmem(40),
        cost_estimate=pl.CostEstimate(
            flops=4 * rows * width * hidden,
            bytes_accessed=rows * hidden * 4 + rows * width * 16 + width * hidden * 4,
            transcendentals=rows * hidden * 2,
        ),
        name="feed_forward",
    )(
        *hbm(mid_n), params, *hbm(own_in, mate_in), own_bias, mate_bias,
        *hbm(own_down, mate_down), *cot, weight,
    )


def product_kernel(a_ref, b_ref, c_ref):
    c_ref[...] = dot(a_ref[...], b_ref[...]).astype(BF16)


def product(a, first, rows, b, block):
    return pl.pallas_call(
        product_kernel,
        grid=(rows // block,),
        in_specs=[pl.BlockSpec((block, a.shape[1]), lambda j: (j + first // block, 0)), whole(b.shape)],
        out_specs=pl.BlockSpec((block, b.shape[1]), lambda j: (j, 0)),
        out_shape=jax.ShapeDtypeStruct((rows, b.shape[1]), BF16),
        compiler_params=vmem(12),
        cost_estimate=pl.CostEstimate(
            flops=2 * rows * a.shape[1] * b.shape[1],
            bytes_accessed=2 * (rows * (a.shape[1] + b.shape[1]) + b.shape[0] * b.shape[1]),
            transcendentals=0,
        ),
        name="weight_gradient",
    )(a, b)


def ffn_back_kernel(
    last, df_ref, slope_ref, wi_ref, wd_ref, h1_t_ref, start_ref, *refs
):
    if last:
        (mid_n_ref, rate_ref, ctx_t_ref, par_ref, gin_ref, db_ref, gown_ref, gmate_ref, ds1_ref,
         da_ref, vec_ref, du, acc) = refs
    else:
        gin_ref, db_ref, acc, du = refs
    step = pl.program_id(0)
    w_in = wi_ref[...]
    w_down = wd_ref[...]

    @pl.when(step == 0)
    def _():
        acc[...] = start_ref[...]

    size = 256
    total = 0.0
    cuts = [slice(at, at + size) for at in range(0, 2 * BLOCK, size)]
    ready = [dot(df_ref[cuts[0], :], w_down, NT)]
    for at, rows in enumerate(cuts):
        if at + 1 < len(cuts):
            ready.append(dot(df_ref[cuts[at + 1], :], w_down, NT))
        d_u = ready[at] * slope_ref[rows, :].astype(F32)
        total = total + jnp.sum(d_u, axis=0, keepdims=True)
        low = d_u.astype(BF16)
        du[rows, :] = low
        acc[rows, :] += dot(low, w_in, NT)
    db_ref[...] = total
    gin_ref[0] = dot(h1_t_ref[...], du[...]).astype(BF16)
    if not last:
        return

    @pl.when(step == pl.num_programs(0) - 1)
    def _():
        sums = [0.0, 0.0]
        gain = par_ref[0:1, :]
        for at in range(0, 2 * BLOCK, size):
            rows = slice(at, at + size)
            d_h1 = acc[rows, :]
            normed = mid_n_ref[rows, :]
            d_s1 = norm_back(d_h1, normed, rate_ref[rows, :], gain)
            ds1_ref[rows, :] = d_s1
            da_ref[rows, :] = d_s1.astype(BF16)
            for n, term in enumerate((d_h1, d_h1 * normed)):
                sums[n] = sums[n] + jnp.sum(term, axis=0, keepdims=True)
        vec_ref[...] = jnp.concatenate(sums + [jnp.zeros((6, gain.shape[1]), F32)], axis=0)
        cut = gown_ref.shape[0]
        gown_ref[...] = dot(ctx_t_ref[:cut, :], da_ref[...]).astype(BF16)
        gmate_ref[...] = dot(ctx_t_ref[cut:, :], da_ref[...]).astype(BF16)


def ffn_back(first, d_f, slope, w_in, w_down, h1_t, start, *rest):
    rows, width = d_f.shape
    hidden = w_in.shape[1]
    tiles = hidden // TILE
    last = len(rest) > 0
    grid_out = [
        pl.BlockSpec((1, width, TILE), lambda j: (j, 0, 0)),
        pl.BlockSpec((1, TILE), lambda j: (0, j)),
    ]
    shapes = [
        jax.ShapeDtypeStruct((tiles, width, TILE), BF16),
        jax.ShapeDtypeStruct((1, hidden), F32),
    ]
    scratch = [pltpu.VMEM((rows, TILE), BF16)]
    if last:
        whole_out = [((width // 2, width), BF16)] * 2 + [
            ((rows, width), F32), ((rows, width), BF16), ((8, width), F32)
        ]
        scratch.append(pltpu.VMEM((rows, width), F32))
    else:
        whole_out = [((rows, width), F32)]
    return pl.pallas_call(
        functools.partial(ffn_back_kernel, last),
        grid=(tiles,),
        in_specs=[
            whole((rows, width)),
            pl.BlockSpec((rows, TILE), lambda j: (0, j + first * tiles)),
            pl.BlockSpec((width, TILE), lambda j: (0, j)),
            pl.BlockSpec((TILE, width), lambda j: (j, 0)),
            whole((width, rows)),
            whole((rows, width)),
        ]
        + [whole(x.shape) for x in rest],
        out_specs=grid_out + [whole(shape) for shape, _ in whole_out],
        out_shape=shapes + [jax.ShapeDtypeStruct(shape, kind) for shape, kind in whole_out],
        scratch_shapes=scratch,
        compiler_params=vmem(32),
        cost_estimate=pl.CostEstimate(
            flops=6 * rows * width * hidden,
            bytes_accessed=rows * hidden * 2 + rows * width * 18 + width * hidden * 6,
            transcendentals=0,
        ),
        name="feed_forward_back",
    )(d_f, *hbm(slope, w_in, w_down), h1_t, start, *hbm(*rest[:-1]), *rest[-1:])


def attend_back_kernel(
    ends, swap_ref, qkv_ref, ctx_t_ref, lse_ref, da_ref, x_t_ref, *refs
):
    step = pl.program_id(0)
    outs = refs[-1 - len(ends) :]
    dqkv = outs[-1]
    w_out = pick(step >= ends[-2], *refs[:2]) if len(ends) > 1 else refs[0][...]
    swap = swap_ref[...] > 0
    scale = LOG2E * HDIM**-0.5

    keys = [qkv_ref[rows, LANES : 2 * LANES] for rows in SLOTS]
    values = [qkv_ref[rows, 2 * LANES :] for rows in SLOTS]
    blocks, units = [], []
    for i, rows in enumerate(SLOTS):
        q = qkv_ref[rows, :LANES]
        k = jnp.where(swap, keys[1 - i], keys[i])
        v = jnp.where(swap, values[1 - i], values[i])
        dctx = dot(da_ref[rows, :], w_out, NT).astype(BF16)
        prod_t = dctx.T.astype(F32) * ctx_t_ref[:, rows].astype(F32)
        blocks.append((rows, q, k, v, k.T, dctx, prod_t))
    for i, (rows, q, k, v, k_t, dctx, prod_t) in enumerate(blocks):
        for n in (0, 1):
            own = head_lanes(n == 0)
            q_n = jnp.where(own, q, jnp.zeros_like(q))
            d_n = jnp.where(own, dctx, jnp.zeros_like(dctx))
            units.append((i, n, q_n, d_n))

    def products(unit):
        i, n, q_n, d_n = unit
        return dot(blocks[i][2], q_n, NT), dot(blocks[i][3], d_n, NT)

    ahead = 1
    ready = [products(unit) for unit in units[:ahead]]
    found = []
    for at, (i, n, q_n, d_n) in enumerate(units):
        if at + ahead < len(units):
            ready.append(products(units[at + ahead]))
        rows, q, k, v, k_t, dctx, prod_t = blocks[i]
        cut = slice(n * HDIM, (n + 1) * HDIM)
        s, d_p = ready[at]
        p = jnp.exp2(s * scale - lse_ref[0, n : n + 1, rows])
        inner = jnp.sum(prod_t[cut], axis=0, keepdims=True)
        ds = (p * (d_p - inner)).astype(BF16)
        dv_n = dot(p.astype(BF16), d_n)
        dk_n = dot(ds, q_n)
        if n == 0:
            dv, dk, dq_t = dv_n, dk_n, [dot(k_t[cut], ds)]
        else:
            dv, dk = dv + dv_n, dk + dk_n
            dq_t.append(dot(k_t[cut], ds))
            dq = jnp.concatenate(dq_t, axis=0).T
            dqkv[rows, :LANES] = (dq * HDIM**-0.5).astype(BF16)
            found.append(((dk * HDIM**-0.5).astype(BF16), dv.astype(BF16)))
    for i, rows in enumerate(SLOTS):
        for at in (0, 1):
            dqkv[rows, (at + 1) * LANES : (at + 2) * LANES] = jnp.where(
                swap, found[1 - i][at], found[i][at]
            )
    grad = dot(x_t_ref[...], dqkv[...]).astype(BF16)
    if len(ends) == 1:
        outs[0][0] = grad
        return
    for first, end, gw_ref in zip((0,) + ends, ends, outs):

        @pl.when(jnp.logical_and(step >= first, step < end))
        def _():
            gw_ref[0] = grad


def attention_back(ends, at, swap_lanes, qkv, ctx_t, lse, w_outs, d_a, x_t):
    rows, width = d_a.shape
    pairs = ends[-1]
    if len(ends) > 1:
        w_at = [lambda p: jnp.maximum(p - ends[-2], 0), lambda p: jnp.minimum(p, ends[-2] - 1)]
    else:
        w_at = [at]

    def w_spec(place):
        return pl.BlockSpec((LANES, width), lambda p: (place(p), 0))

    def spec(first, end):
        return pl.BlockSpec(
            (1, width, 3 * LANES), lambda p: (jnp.clip(p - first, 0, end - first - 1), 0, 0)
        )

    parts = list(zip((0,) + ends, ends))
    return pl.pallas_call(
        functools.partial(attend_back_kernel, ends),
        grid=(pairs,),
        in_specs=[
            pl.BlockSpec((1, LANES), lambda p: (0, at(p))),
            pl.BlockSpec((rows, 3 * LANES), lambda p: (0, at(p))),
            pl.BlockSpec((LANES, rows), lambda p: (at(p), 0)),
            pl.BlockSpec((1, 2, rows), lambda p: (at(p), 0, 0)),
            whole((rows, width)),
            whole((width, rows)),
        ]
        + [w_spec(place) for place in w_at],
        out_specs=[spec(*part) for part in parts]
        + [pl.BlockSpec((rows, 3 * LANES), lambda p: (0, p))],
        out_shape=[
            jax.ShapeDtypeStruct((end - first, width, 3 * LANES), BF16) for first, end in parts
        ]
        + [pltpu.HBM((rows, pairs * 3 * LANES), BF16)],
        compiler_params=vmem(24),
        cost_estimate=pl.CostEstimate(
            flops=8 * rows * width * pairs * LANES + 4 * pairs * 10 * BLOCK * BLOCK * 256,
            bytes_accessed=rows * width * 14,
            transcendentals=4 * pairs * BLOCK * BLOCK,
        ),
        name="attention_backward",
    )(swap_lanes, *hbm(qkv, ctx_t), lse, d_a, *hbm(x_t, *w_outs))


def input_kernel(first_ref, later_ref, mate_ref, wq_ref, wk_ref, wv_ref, mq_ref, mk_ref, mv_ref, start_ref,
                 kept_ref, given_ref, acc):
    step = pl.program_id(0)
    w = jnp.concatenate([wq_ref[...], wk_ref[...], wv_ref[...]], axis=1)
    m = jnp.concatenate([mq_ref[...], mk_ref[...], mv_ref[...]], axis=1)

    @pl.when(step == 0)
    def _():
        acc[...] = start_ref[...]

    for rows in SLOTS:
        own = jnp.where(step == 0, first_ref[rows, :], later_ref[rows, :])
        acc[rows, :] += dot(own, w, NT) + dot(mate_ref[rows, :], m, NT)

    @pl.when(step == pl.num_programs(0) - 1)
    def _():
        kept_ref[...] = acc[:BLOCK, :]
        given_ref[...] = acc[BLOCK:, :].astype(BF16)


def input_gradient(early, late, own_w, mate_w, start):
    rows, width = start.shape
    pairs = early.shape[1] // (3 * LANES) - 1
    part = (rows, 3 * LANES)
    w_spec = pl.BlockSpec((width, LANES), lambda p: (0, p))
    return pl.pallas_call(
        input_kernel,
        grid=(pairs,),
        in_specs=[
            pl.BlockSpec(part, lambda p: (0, pairs)),
            pl.BlockSpec(part, lambda p: (0, jnp.maximum(p - 1, 0))),
            pl.BlockSpec(part, lambda p: (0, p)),
        ]
        + [w_spec] * 6 + [whole((rows, width))],
        out_specs=[whole((BLOCK, width))] * 2,
        out_shape=[
            jax.ShapeDtypeStruct((BLOCK, width), F32), jax.ShapeDtypeStruct((BLOCK, width), BF16)
        ],
        scratch_shapes=[pltpu.VMEM((rows, width), F32)],
        compiler_params=vmem(24),
        cost_estimate=pl.CostEstimate(
            flops=12 * rows * width * pairs * LANES,
            bytes_accessed=rows * width * 14,
            transcendentals=0,
        ),
        name="input_gradient",
    )(*hbm(early, late, early, *own_w, *mate_w), start)


def halves(x, place):
    rows = x.shape[0] // 2
    return (
        lax.dynamic_slice_in_dim(x, place * rows, rows, 0),
        lax.dynamic_slice_in_dim(x, (1 - place) * rows, rows, 0),
    )


def joined(mine, other, place):
    return jnp.where(
        place == 0,
        jnp.concatenate([mine, other], axis=0),
        jnp.concatenate([other, mine], axis=0),
    )


def add_low(a, b):
    return (a.astype(F32) + b.astype(F32)).astype(BF16)


def after(x, *others):
    return lax.optimization_barrier((x, others))[0]


def spots(left, bit, value):
    low = sum(other < bit for other in left)
    count = 1 << (len(left) - 1)
    return [((n >> low) << (low + 1) | n & ((1 << low) - 1)) + (value << low) for n in range(count)]


class Streams:
    def __init__(self, refs, rows):
        self.refs, self.rows = refs, rows

    def at(self, stream, spot):
        if len(self.refs) == 2:
            return self.refs[stream].at[spot]
        first = sum(self.rows[:stream])
        return self.refs[0].at[spot, first : first + self.rows[stream]]


class TokSum:
    def __init__(self, streams, own, got, extra=None, finish=None, alone=False):
        self.size = lax.axis_size("tok")
        bits = self.size.bit_length() - 1
        self.there = [(0, 1), (1, 0)] + [(bit, bit) for bit in range(2, bits)]
        self.left = [list(reversed(range(bits)))] * 2
        self.job = 0
        self.alone = alone
        self.extra, self.finish = extra, finish
        units = [0] * len(own)
        for stream in streams:
            for n, first, rows in stream:
                units[n] = math.gcd(units[n], first, rows // self.size)
        self.items = [
            [(n, first // units[n], rows // self.size // units[n], units[n]) for n, first, rows in stream]
            for stream in streams
        ]
        self.rows = [sum(rows // self.size for _, _, rows in stream) for stream in streams]
        self.width = own[0].shape[-1]
        self.inputs = [
            x.reshape(-1, unit, self.width) for xs in (own, got) for x, unit in zip(xs, units)
        ]

    def shapes(self, count, together):
        rows = [sum(self.rows)] if together else self.rows
        return [jax.ShapeDtypeStruct((count, row, self.width), BF16) for row in rows]

    def work(self):
        steps = len(self.there)
        job, self.job = self.job, self.job + 1
        if job <= steps:
            return self.adding(job, steps)
        return self.joining(2 * steps - job)

    def adding(self, job, steps):
        inputs, rows, left = self.inputs, self.rows, self.left
        extra = self.extra if job == steps else None
        if job < steps:
            bits = self.there[job]
            together = bits[0] == bits[1]
            half = self.shapes(1 << (len(left[0]) - 1), together)
            shapes = [pltpu.VMEM(x.shape, x.dtype) for x in half] + half
            self.left = [[b for b in mine if b != bit] for mine, bit in zip(left, bits)]
        else:
            bits = None
            if extra is not None:
                self.rows = [row + x.shape[0] for row, x in zip(rows, extra)]
                inputs = inputs + list(extra)
            shapes = self.shapes(1, True)
        new_rows = self.rows
        self.sent = len(shapes) // 2 if job < steps else 0

        def body(place, ins, outs):
            if extra is not None:
                ins, extras = ins[:-2], ins[-2:]
            count = len(ins) // 2

            def sums(stream, spot):
                if job > 0:
                    found = [Streams(ins[:count], rows), Streams(ins[count:], rows)]
                    a, b = (part.at(stream, spot)[...] for part in found)
                    return [(0, rows[stream], add_low(a, b))]
                first, found = 0, []
                for n, base, count_each, unit in self.items[stream]:
                    for piece in range(count_each):
                        block = base + spot * count_each + piece
                        found.append((first, unit, add_low(ins[n][block], ins[count + n][block])))
                        first += unit
                return found

            for stream in (0, 1):
                if bits is None:
                    ref = Streams(outs, new_rows).at(stream, 0)
                    ((_, row, value),) = sums(stream, 0)
                    ref[:row, :] = value
                    if extra is not None:
                        ref[row:, :] = extras[stream][...]
                    continue
                mine = place >> bits[stream] & 1
                split = len(outs) // 2
                for which, value in ((0, mine), (1, 1 - mine)):
                    target = Streams(outs[which * split : (which + 1) * split], rows)
                    for n, spot in enumerate(spots(left[stream], bits[stream], value)):
                        ref = target.at(stream, n)
                        for first, row, total in sums(stream, spot):
                            ref[first : first + row, :] = total

        return inputs, shapes, body

    def joining(self, step):
        inputs, rows = self.inputs, self.rows
        bits = self.there[step]
        before = self.left
        self.left = left = [sorted(have + [bit], reverse=True) for have, bit in zip(before, bits)]
        self.sent = 0
        if step == 0:
            shapes, write = self.finish(rows)
        else:
            then = self.there[step - 1]
            shapes = self.shapes(1 << len(left[0]), then[0] == then[1])

        def body(place, ins, outs):
            count = len(ins) // 2
            found = [Streams(ins[:count], rows), Streams(ins[count:], rows)]
            for stream in (0, 1):
                bit = bits[stream]
                mine = place >> bit & 1
                if step == 0:
                    low = sum(other < bit for other in left[stream])
                    for spot in range(1 << len(left[stream])):
                        n = (spot >> (low + 1)) << low | spot & ((1 << low) - 1)
                        kept, new = (part.at(stream, n)[...] for part in found)
                        write(outs, stream, spot, jnp.where(mine == (spot >> low & 1), kept, new))
                    continue
                for part, value in zip(found, (mine, 1 - mine)):
                    for n, spot in enumerate(spots(left[stream], bit, value)):
                        Streams(outs, rows).at(stream, spot)[...] = part.at(stream, n)[...]

        return inputs, shapes, body

    def take(self, outs):
        steps = len(self.there)
        if self.job > 2 * steps:
            self.found = outs
            return []
        kept, sent = (outs[: self.sent], outs[self.sent :]) if self.sent else (outs, outs)
        if self.job == steps + 1 and self.alone:
            self.piece = [sent[0].reshape(sent[0].shape[1:])]
            return sent
        step = self.job - 1 if self.job <= steps else 2 * steps - self.job
        got = [swap_bit(x, "tok", bit) for x, bit in zip(sent, self.there[step])]
        self.inputs = list(kept) + got
        return sent


def gather_rest(one):
    spread = lax.all_gather(one.piece[0], "tok", axis=0)
    one.job = 2 * len(one.there) + 1
    rows = one.rows
    shapes, write = one.finish(rows)

    def kernel(x_ref, *outs):
        for spot in range(x_ref.shape[0]):
            write(outs, 0, spot, x_ref[spot, : rows[0]])
            write(outs, 1, spot, x_ref[spot, rows[0] :])

    one.found = pl.pallas_call(
        kernel,
        in_specs=[pl.BlockSpec(memory_space=pltpu.VMEM)],
        out_specs=[pl.BlockSpec(memory_space=pltpu.VMEM)] * len(shapes),
        out_shape=shapes,
        compiler_params=vmem(32),
        name="sum_spread",
    )(spread)


class PlainSum:
    def __init__(self, streams, own, got, extra=None, finish=None, alone=False):
        whole = [
            lax.psum(a.astype(F32) + b.astype(F32), "tok").reshape(-1, a.shape[-1])
            for a, b in zip(own, got)
        ]
        self.found = [
            [whole[n][first : first + rows] for n, first, rows in stream] for stream in streams
        ]


def advance(sums, *others):
    if not isinstance(sums[0], TokSum):
        return []
    place = after(lax.axis_index("tok").astype(jnp.int32).reshape(1), *others)
    works = [one.work() for one in sums]

    def kernel(place_ref, *refs):
        place = place_ref[0]
        ins = refs[: sum(len(work[0]) for work in works)]
        outs = refs[len(ins) :]
        for inputs, shapes, body in works:
            body(place, ins[: len(inputs)], outs[: len(shapes)])
            ins, outs = ins[len(inputs) :], outs[len(shapes) :]

    inputs = [x for work in works for x in work[0]]
    shapes = [x for work in works for x in work[1]]
    size = 2 * sum(math.prod(x.shape) for x in inputs + shapes)
    outs = pl.pallas_call(
        kernel,
        in_specs=[pl.BlockSpec(memory_space=pltpu.SMEM)]
        + [pl.BlockSpec(memory_space=pltpu.VMEM)] * len(inputs),
        out_specs=[pl.BlockSpec(memory_space=pltpu.VMEM)] * len(shapes),
        out_shape=shapes,
        compiler_params=vmem(20),
        cost_estimate=pl.CostEstimate(flops=size, bytes_accessed=size, transcendentals=0),
        name="sum_step",
    )(place, *inputs)
    sent = []
    for one, work in zip(sums, works):
        sent += one.take(outs[: len(work[1])])
        outs = outs[len(work[1]) :]
    return sent


def body(
    tokens,
    cotangent,
    block_source,
    mask_index,
    mask_count,
    w_query,
    w_key,
    w_value,
    w_output,
    mid_gain,
    mid_shift,
    w_inner,
    bias_inner,
    w_outer,
    bias_outer,
    end_gain,
    end_shift,
):
    tok_place = lax.axis_index("tok")
    head_place = lax.axis_index("head")
    half = tok_place % 2
    width = tokens.shape[1]

    def mate(x):
        return swap_bit(x, "head", 0)

    kept, given = halves(tokens, half)
    cot_kept, cot_given = halves(cotangent, half)
    x_got = swap_bit(given, "tok", 0)
    own_w = (w_query, w_key, w_value)
    mate_w = tuple(mate(w) for w in own_w)
    mate_out = mate(w_output)
    mate_in = mate(w_inner)
    own_bias = bias_inner[None, :]
    mate_bias = mate(own_bias)

    sequence = tok_place // 2 * PAIR_SEQS + 2 * head_place + half
    source = lax.dynamic_slice_in_dim(block_source, sequence, 1, 0)[0, :, 0]
    per_half = GROUPS // 2
    flags = jnp.concatenate(
        [
            lax.dynamic_slice_in_dim(source, head_place * per_half, per_half, 0),
            lax.dynamic_slice_in_dim(source, (1 - head_place) * per_half, per_half, 0),
        ]
    )
    swap_lanes = jnp.repeat(flags, HEADS // GROUPS * HDIM)[None, :]
    positions = lax.dynamic_slice_in_dim(mask_index, sequence, 1, 0)[0]
    count = lax.dynamic_slice_in_dim(mask_count, sequence, 1, 0)[0]
    within = jnp.arange(BLOCK)
    places = jnp.concatenate([half * BLOCK + within, (1 - half) * BLOCK + within])
    live = jnp.arange(positions.shape[0]) < count
    hits = jnp.any((positions[None, :] == places[:, None]) & live[None, :], axis=1)
    weight = (1.0 + 3.0 * hits.astype(F32))[:, None]
    params = jnp.stack(
        [mid_gain, mid_shift, bias_outer, end_gain, end_shift] + [jnp.zeros_like(mid_gain)] * 3
    )
    mate_down = mate(after(w_outer, weight, swap_lanes, cot_given, params))

    qkv, lse, ctx_t, x_t, mid_n, mid_rate = attention(
        swap_lanes, (kept, after(x_got, swap_lanes, weight, params, cot_kept)), own_w, mate_w,
        w_output, mate_out,
    )
    cot_got = swap_bit(after(cot_given, x_got), "tok", 0)
    act_t, slope, h1_t, out, d_s2, d_f, end_vec, g_mate = ffn(
        mid_n, params, w_inner, mate_in, own_bias, mate_bias, w_outer, mate_down,
        (cot_kept, cot_got), weight,
    )

    hidden = w_inner.shape[1]
    cut = w_output.shape[0]
    pairs = cut // LANES

    def side_by_side(g):
        return jnp.concatenate([g[:, n : n + COLS] for n in range(0, width, COLS)], axis=0)

    rest = width // 2

    def finish_down(rows):
        def write(outs, stream, spot, value):
            outs[0][stream, spot] = value.astype(F32)

        return [jax.ShapeDtypeStruct((2, lax.axis_size("tok"), rows[0], width), F32)], write

    def finish_inner(rows):
        size = lax.axis_size("tok")

        def write(outs, stream, spot, value):
            value = value.astype(F32)
            outs[0][spot, :, stream * width : (stream + 1) * width] = value[: rows[0]]
            if stream == 1:
                outs[1][spot] = value[rows[0] :]

        return [
            jax.ShapeDtypeStruct((size, rows[0], 2 * width), F32),
            jax.ShapeDtypeStruct((size, rows[1] - rows[0], width), F32),
        ], write

    size = lax.axis_size("tok")
    fits = size & (size - 1) == 0 and size >= 4 and rest % (8 * size) == 0
    Sum = TokSum if fits else PlainSum

    got = mate(g_mate)
    mine = product(act_t, 0, hidden, d_f, BLOCK)
    cut = hidden // 2
    down = Sum([[(0, 0, cut)], [(0, cut, cut)]], [mine], [got], finish=finish_down, alone=False)
    sent = advance([down], mine)
    gi_mate, gb_mate, d_h1 = ffn_back(
        1, after(d_f, sent), slope, mate_in, mate_down, h1_t, d_s2
    )
    sent = advance([down], gi_mate)
    out_got = swap_bit(after(out[BLOCK:], sent), "tok", 0)
    got_in = mate(after(gi_mate, sent))
    gi_own, gb_own, go_own, go_mate, d_s1, d_a, mid_vec = ffn_back(
        0, after(d_f, sent), slope, w_inner, w_outer, h1_t, d_h1, mid_n, mid_rate, ctx_t, params
    )
    got_out = mate(after(go_mate, down.inputs[-2:], out_got) if fits else go_mate)
    inner = Sum(
        [[(0, 0, width)], [(0, width, width), (1, 0, rest)]],
        [gi_own, go_own], [got_in, got_out], finish=finish_inner, alone=False,
    )
    sent = advance([inner, down], gi_own)
    gw_mate, gw_mates, gw_own, dp_early = attention_back(
        (1, pairs, pairs + 1), lambda p: jnp.where(p < pairs, p + pairs, 0), swap_lanes, qkv, ctx_t,
        lse, (w_output, mate_out), after(d_a, sent), x_t,
    )
    sent = advance([inner, down], gw_own)
    gw_got, gw_gots = (mate(x) for x in after((gw_mate, gw_mates), sent))

    gb_own, gb_mate = gb_own.reshape(-1, width), gb_mate.reshape(-1, width)
    own_rows = gb_own.shape[0]
    small = jnp.concatenate([end_vec[:3], mid_vec[:2], gb_own, gb_mate], axis=0)
    theirs = mate(small)
    small = jnp.concatenate(
        [
            small[:5] + theirs[:5],
            small[5 : 5 + own_rows] + theirs[5 + own_rows :],
            jnp.zeros((1, width), F32),
        ],
        axis=0,
    )
    high = small.astype(BF16)
    low = (small - high.astype(F32)).astype(BF16)
    high, low = side_by_side(high), side_by_side(low)

    gw_owns, dp_late = attention_back(
        (pairs - 1,), lambda p: p + 1, swap_lanes, qkv, ctx_t, lse, (w_output,), after(d_a, sent), x_t
    )
    head = (pairs * width // size + 31) // 32 * 16 * size - width

    def finish_last(rows):
        def write(outs, stream, spot, value):
            value = value.astype(F32)
            extra = high.shape[0]
            count = rows[stream] - extra
            pieces = [(0, spot * count + width + head, count)]
            if stream == 0:
                one = width // size
                pieces = [(0, spot * one, one), (one, width + spot * (count - one), count - one)]
            for done, first, length in pieces:
                while length > 0:
                    p, row = divmod(first, width)
                    step = min(length, width - row)
                    for at in range(3):
                        outs[at][row : row + step, p * LANES : (p + 1) * LANES] = value[
                            done : done + step, at * LANES : (at + 1) * LANES
                        ]
                    done, first, length = done + step, first + step, length - step
            if stream == 0 and spot == 0:
                outs[3][...] = value[count:]
            else:
                outs[3][...] += value[count:]

        return [jax.ShapeDtypeStruct((width, pairs * LANES), F32)] * 3 + [
            jax.ShapeDtypeStruct(high.shape, F32)
        ], write

    rows = (pairs - 1) * width
    last = Sum(
        [[(0, 0, width), (1, 0, head)], [(1, head, rows - head)]],
        [x.reshape(-1, 3 * LANES) for x in (gw_own, gw_owns)],
        [x.reshape(-1, 3 * LANES) for x in (gw_got, gw_gots)],
        extra=(high, low), finish=finish_last,
    )
    sent = advance([last, inner, down], gw_owns)
    out = joined(out[:BLOCK], out_got, half)
    dx_kept, dx_given = input_gradient(dp_early, after(dp_late, sent), own_w, mate_w, d_s1)
    dx_got = []
    if fits:
        while last.job <= 2 * len(last.there):
            for one in (inner, down):
                if one.alone and one.job == len(one.there) + 1:
                    gather_rest(one)
            sums = [one for one in (last, inner, down) if one.job <= 2 * len(one.there)]
            others = [dx_given] if last.job == 1 else []
            if last.job in (2, 3):
                first = (last.job - 2) * (BLOCK // 2)
                part = dx_given[first : first + BLOCK // 2]
                others = [swap_bit(after(part, last.inputs[0]), "tok", 0)]
                dx_got += others
            advance(sums, *others)
        g_down, (g_in, g_out), (g_query, g_key, g_value, sums) = (
            down.found[0], inner.found, last.found
        )
        small = jnp.concatenate([sums[: small.shape[0]], sums[small.shape[0] :]], axis=1)
    else:
        dx_got = [swap_bit(dx_given, "tok", 0)]
        g_down = jnp.concatenate([down.found[0][0], down.found[1][0]], axis=0)
        g_in = jnp.concatenate([inner.found[0][0], inner.found[1][0]], axis=1)
        g_out = inner.found[1][1]
        whole_w = jnp.concatenate(last.found[0] + last.found[1], axis=0)
        whole_w = whole_w.reshape(pairs, width, 3, LANES)
        g_query, g_key, g_value = (
            jnp.concatenate([whole_w[p, :, at] for p in range(pairs)], axis=1) for at in range(3)
        )
        small = lax.psum(small, "tok")
    dx_got = jnp.concatenate(dx_got, axis=0).astype(F32)
    grad_tokens = joined(dx_kept, dx_got, half)
    g_down = g_down.reshape(hidden, width)
    g_in = g_in.reshape(width, hidden)
    g_out = g_out.reshape(rest, width)

    return (
        out,
        grad_tokens,
        g_query,
        g_key,
        g_value,
        g_out,
        small[4],
        small[3],
        g_in,
        small[5 : 5 + own_rows].reshape(-1),
        g_down,
        small[2],
        small[1],
        small[0],
    )


def solution(mesh):
    rows = P(("tok", "head"), None)
    return jax.shard_map(
        body,
        mesh=mesh,
        in_specs=(
            rows,
            rows,
            P(),
            P(),
            P(),
            P(None, "head"),
            P(None, "head"),
            P(None, "head"),
            P("head", None),
            P(),
            P(),
            P(None, "head"),
            P("head"),
            P("head", None),
            P(),
            P(),
            P(),
        ),
        out_specs=(
            rows,
            rows,
            P(None, "head"),
            P(None, "head"),
            P(None, "head"),
            P("head", None),
            P(),
            P(),
            P(None, "head"),
            P("head"),
            P("head", None),
            P(),
            P(),
            P(),
        ),
        check_vma=False,
    )
```

profile of v0, /device:TPU:0, one launch (start us, length us, event | category | flops | bytes accessed | tf_op | source)
XLA Modules:
  0.0 285.0 jit_solution(13340730078593430873)
XLA Ops:
  2.3 3.0 %collective-permute-start = (bf16[512,768]{1,0:T(8,128)(2,1)S(1)}, bf16[512,768]{1,0:T(8,128)(2,1)S(1)}, u32[]{:S(2)}, u32[]{:S(2)}) collective-permute-start(bf16[512,768]{1,0:T(8,128)(2,1)S(1)} %get-tuple-element.257), channel_id=1, source_target_pairs={{0,2},{2,0},{4,6},{6,4},{8,10},{10,8},{12,14},{14,12},{16,18},{18,... | collective-permute-start | bytes 2359304 | tf_op jit(solution)/shard_map/ppermute | solution.py:25
  11.1 5.4 %collective-permute-done.1.mq_ref = bf16[768,384]{1,0:T(8,128)(2,1)S(1)} collective-permute-done((bf16[768,384]{1,0:T(8,128)(2,1)}, bf16[768,384]{1,0:T(8,128)(2,1)S(1)}, u32[]{:S(2)}, u32[]{:S(2)}) %collective-permute-start.1) | collective-permute-done | bytes 589856 | tf_op jit(solution)/shard_map/ppermute | solution.py:25
  16.6 6.2 %collective-permute-done.xb_ref = bf16[512,768]{1,0:T(8,128)(2,1)S(1)} collective-permute-done((bf16[512,768]{1,0:T(8,128)(2,1)S(1)}, bf16[512,768]{1,0:T(8,128)(2,1)S(1)}, u32[]{:S(2)}, u32[]{:S(2)}) %collective-permute-start) | collective-permute-done | bytes 786464 | tf_op jit(solution)/shard_map/ppermute | solution.py:25
  25.4 21.8 %attention_forward.1 = (bf16[1024,2304]{1,0:T(8,128)(2,1)}, f32[6,2,1024]{2,1,0:T(2,128)S(1)}, bf16[768,1024]{1,0:T(8,128)(2,1)}, bf16[768,1024]{1,0:T(8,128)(2,...) custom-call(s32[1,768]{1,0:T(1,128)S(1)} %broadcast_in_dim_reshape.3.swap_ref, ...), custom_call_target="tpu_custom_call" | custom-call | flops 11274289152 | bytes 18874368 | tf_op jit(solution)/shard_map/attention_forward/pallas_call | solution.py:154
  47.3 29.7 %feed_forward.1 = (bf16[1536,1024]{1,0:T(8,128)(2,1)S(1)}, bf16[1024,3072]{1,0:T(8,128)(2,1)}, bf16[768,1024]{1,0:T(8,128)(2,1)S(1)}, bf16[1024,768]{1,0:T(8,128...) custom-call(f32[1024,768]{1,0:T(8,128)} %get-tuple-element.131.mid_n, ...), custom_call_target="tpu_custom_call" | custom-call | flops 9663676416 | bytes 34603008 | tf_op jit(solution)/shard_map/feed_forward/pallas_call | solution.py:265
  77.1 3.0 %weight_gradient.1 = bf16[1536,768]{1,0:T(8,128)(2,1)S(1)} custom-call(bf16[1536,1024]{1,0:T(8,128)(2,1)S(1)} %get-tuple-element.136.a_ref, bf16[1024,768]{1,0:T(8,128)(2,1)S(1)} %get-tuple-element.155.b_ref.df_ref), custom_call_target="tpu_custom_call" | custom-call | flops 2415919104 | bytes 7077888 | tf_op jit(solution)/shard_map/weight_gradient/pallas_call | solution.py:324
  85.2 10.4 %feed_forward_back.2 = (bf16[2,768,768]{2,1,0:T(8,128)(2,1)S(1)}, f32[1,1536]{1,0:T(1,128)S(1)}, f32[1024,768]{1,0:T(8,128)S(1)}) custom-call(bf16[1024,768]{1,0:T(8,128)(2,1)S(1)} %get-tuple-element.155.b_ref.df_ref, bf16[1024,3072]{1,0:T(8,128)(2,1)} %get-tuple-element.142.slope_ref, bf16[768,1536]{1,0:T(8,128)(2,1)} %collective-permute-done.5.mi_ref.wi_ref, ...), custom_call_target="tpu_custom_call" | custom-call | flops 7247757312 | bytes 24379392 | tf_op jit(solution)/shard_map/feed_forward_back/pallas_call | solution.py:413
  103.7 15.6 %feed_forward_back.3 = (bf16[2,768,768]{2,1,0:T(8,128)(2,1)S(1)}, f32[1,1536]{1,0:T(1,128)S(1)}, bf16[384,768]{1,0:T(8,128)(2,1)S(1)}, bf16[384,768]{1,0:T(8,128...) custom-call(bf16[1024,768]{1,0:T(8,128)(2,1)S(1)} %get-tuple-element.155.b_ref.df_ref, ...), custom_call_target="tpu_custom_call" | custom-call | flops 7247757312 | bytes 24379392 | tf_op jit(solution)/shard_map/feed_forward_back/pallas_call | solution.py:413
  119.3 7.1 %collective-permute-done.15.refs_7_ = bf16[4,48,768]{2,1,0:T(8,128)(2,1)S(1)} collective-permute-done((bf16[4,48,768]{2,1,0:T(8,128)(2,1)S(1)}, bf16[4,48,768]{2,1,0:T(8,128)(2,1)S(1)}, u32[]{:S(2)}, u32[]{:S(2)}) %collective-permute-start.15) | collective-permute-done | bytes 294944 | tf_op jit(solution)/shard_map/ppermute | solution.py:25
  132.9 19.9 %attention_backward.2 = (bf16[1,768,384]{2,1,0:T(8,128)(2,1)S(1)}, bf16[2,768,384]{2,1,0:T(8,128)(2,1)S(1)}, bf16[1,768,384]{2,1,0:T(8,128)(2,1)S(1)}, bf16[1024,1536]{1,0:T(8,128)(2,1)}) custom-call(s32[1,768]{1,0:T(1,128)S(1)} %broadcast_in_dim_reshape.3.swap_ref, bf16[1024,2304]{1,0:T(8,128)(2,1)} %get-tuple-element.152.qkv_ref, ...), custom_call_target="tpu_custom_call" | custom-call | flops 13958643712 | bytes 11010048 | tf_op jit(solution)/shard_map/attention_backward/pallas_call | solution.py:524
  153.4 2.6 collective-permute-start.24
  158.7 10.2 %attention_backward.3 = (bf16[2,768,384]{2,1,0:T(8,128)(2,1)S(1)}, bf16[1024,768]{1,0:T(8,128)(2,1)}) custom-call(s32[1,768]{1,0:T(1,128)S(1)} %broadcast_in_dim_reshape.3.swap_ref, bf16[1024,2304]{1,0:T(8,128)(2,1)} %get-tuple-element.152.qkv_ref, bf16[768,1024]{1,0:T(8,128)(2,1)} %get-tuple-element.153.refs_2_.ctx_t_ref, ...), custom_call_target="tpu_custom_call" | custom-call | flops 6979321856 | bytes 11010048 | tf_op jit(solution)/shard_map/attention_backward/pallas_call | solution.py:524
  173.0 8.7 %input_gradient.1 = (f32[512,768]{1,0:T(8,128)S(1)}, bf16[512,768]{1,0:T(8,128)(2,1)S(1)}) custom-call(bf16[1024,1536]{1,0:T(8,128)(2,1)} %get-tuple-element.172.first_ref.mate_ref, bf16[1024,768]{1,0:T(8,128)(2,1)} %get-tuple-element.196.later_ref, bf16[1024,1536]{1,0:T(8,128)(2,1)} %get-tuple-element.172.first_ref.mate_ref, bf16[768,384]{1,0:T(8,128)(2,1)} %wq_ref.3, ...), custom_call_target="tpu_custom_call" | custom-call | flops 3623878656 | bytes 11010048 | tf_op jit(solution)/shard_map/input_gradient/pallas_call | solution.py:577
  192.5 4.9 %collective-permute-done.29 = bf16[256,768]{1,0:T(8,128)(2,1)} collective-permute-done((bf16[256,768]{1,0:T(8,128)(2,1)}, bf16[256,768]{1,0:T(8,128)(2,1)}, u32[]{:S(2)}, u32[]{:S(2)}) %collective-permute-start.29) | collective-permute-done | bytes 393248 | tf_op jit(solution)/shard_map/ppermute | solution.py:25
  206.8 5.0 %collective-permute-done.34 = bf16[256,768]{1,0:T(8,128)(2,1)S(1)} collective-permute-done((bf16[256,768]{1,0:T(8,128)(2,1)S(1)}, bf16[256,768]{1,0:T(8,128)(2,1)S(1)}, u32[]{:S(2)}, u32[]{:S(2)}) %collective-permute-start.34) | collective-permute-done | bytes 393248 | tf_op jit(solution)/shard_map/ppermute | solution.py:25
  212.5 3.0 %collective-permute-done.38.refs_7_ = bf16[4,48,768]{2,1,0:T(8,128)(2,1)S(1)} collective-permute-done((bf16[4,48,768]{2,1,0:T(8,128)(2,1)S(1)}, bf16[4,48,768]{2,1,0:T(8,128)(2,1)S(1)}, u32[]{:S(2)}, u32[]{:S(2)}) %collective-permute-start.38) | collective-permute-done | bytes 294944 | tf_op jit(solution)/shard_map/ppermute | solution.py:25
  221.1 4.9 %collective-permute-done.39.refs_1_ = bf16[1,144,384]{2,1,0:T(8,128)(2,1)S(1)} collective-permute-done((bf16[1,144,384]{2,1,0:T(8,128)(2,1)S(1)}, bf16[1,144,384]{2,1,0:T(8,128)(2,1)S(1)}, u32[]{:S(2)}, u32[]{:S(2)}) %collective-permute-start.39) | collective-permute-done | bytes 110624 | tf_op jit(solution)/shard_map/ppermute | solution.py:25
  228.7 2.6 sum_step.21
  236.3 5.0 %collective-permute-done.44.refs_1_ = bf16[1,176,384]{2,1,0:T(8,128)(2,1)S(1)} collective-permute-done((bf16[1,176,384]{2,1,0:T(8,128)(2,1)S(1)}, bf16[1,176,384]{2,1,0:T(8,128)(2,1)S(1)}, u32[]{:S(2)}, u32[]{:S(2)}) %collective-permute-start.44) | collective-permute-done | bytes 135200 | tf_op jit(solution)/shard_map/ppermute | solution.py:25
  245.1 5.0 %collective-permute-done.47.refs_1_ = bf16[2,176,384]{2,1,0:T(8,128)(2,1)S(1)} collective-permute-done((bf16[2,176,384]{2,1,0:T(8,128)(2,1)S(1)}, bf16[2,176,384]{2,1,0:T(8,128)(2,1)S(1)}, u32[]{:S(2)}, u32[]{:S(2)}) %collective-permute-start.47) | collective-permute-done | bytes 270368 | tf_op jit(solution)/shard_map/ppermute | solution.py:25
  252.5 6.1 %collective-permute-done.49.refs_5_ = bf16[8,72,768]{2,1,0:T(8,128)(2,1)S(1)} collective-permute-done((bf16[8,72,768]{2,1,0:T(8,128)(2,1)S(1)}, bf16[8,72,768]{2,1,0:T(8,128)(2,1)S(1)}, u32[]{:S(2)}, u32[]{:S(2)}) %collective-permute-start.49) | collective-permute-done | bytes 884768 | tf_op jit(solution)/shard_map/ppermute | solution.py:25
  258.6 3.1 %sum_step.23 = (bf16[4,96,384]{2,1,0:T(8,128)(2,1)S(1)}, bf16[4,80,384]{2,1,0:T(8,128)(2,1)S(1)}, f32[16,48,1536]{2,1,0:T(8,128)}, f32[16,24,768]{2,1,0:T(8,128)}) custom-call(s32[1]{0:T(128)} %bitcast.3.place_ref, bf16[2,176,384]{2,1,0:T(8,128)(2,1)S(1)} %get-tuple-element.232.refs_0_, bf16[2,176,384]{2,1,0:T(8,128)(2,1)S(1)} %collective-permute-done.47.refs_1_, ...), custom_call_target="tpu_custom_call" | custom-call | flops 6979584 | bytes 6979584 | tf_op jit(solution)/shard_map/sum_step/pallas_call | solution.py:826
  263.4 8.1 %collective-permute-done.51.refs_3_ = bf16[4,80,384]{2,1,0:T(8,128)(2,1)S(1)} collective-permute-done((bf16[4,80,384]{2,1,0:T(8,128)(2,1)S(1)}, bf16[4,80,384]{2,1,0:T(8,128)(2,1)S(1)}, u32[]{:S(2)}, u32[]{:S(2)}) %collective-permute-start.51) | collective-permute-done | bytes 245792 | tf_op jit(solution)/shard_map/ppermute | solution.py:25
  273.3 3.5 %maximum_select_fusion.1 = bf16[1024,768]{1,0:T(8,128)(2,1)} fusion(bf16[512,768]{1,0:T(8,128)(2,1)} %copy-done.5, bf16[512,768]{1,0:T(8,128)(2,1)} %get-tuple-element.253, pred[]{:T(512)S(6)} %eq.21), kind=kLoop, calls=%fused_computation.1 | loop fusion | flops 7077888 | bytes 3145729 | tf_op jit(solution)/shard_map/jit(_where)/select_n | solution.py:610
  (188 shorter events, 88.5 us)
Async XLA Ops:
  2.3 20.5 %collective-permute-start = (bf16[512,768]{1,0:T(8,128)(2,1)S(1)}, bf16[512,768]{1,0:T(8,128)(2,1)S(1)}, u32[]{:S(2)}, u32[]{:S(2)}) collective-permute-start(bf16[512,768]{1,0:T(8,128)(2,1)S(1)} %get-tuple-element.257), channel_id=1, source_target_pairs={{0,2},{2,0},{4,6},{6,4},{8,10},{10,8},{12,14},{14,12},{16,18},{18,... | collective-permute-start | bytes 2359304 | tf_op jit(solution)/shard_map/ppermute | solution.py:25
  10.0 37.3 %collective-permute-start.7 = (bf16[1536,768]{1,0:T(8,128)(2,1)}, bf16[1536,768]{1,0:T(8,128)(2,1)}, u32[]{:S(2)}, u32[]{:S(2)}) collective-permute-start(bf16[1536,768]{1,0:T(8,128)(2,1)} %wd_ref.3), channel_id=1, source_target_pairs={{0,1},{1,0},{2,3},{3,2},{4,5},{5,4},{6,7},{7,6},{8,9},{9,8},{10,11... | collective-permute-start | bytes 7077896 | tf_op jit(solution)/shard_map/ppermute | solution.py:25
  10.0 37.2 %collective-permute-start.5 = (bf16[768,1536]{1,0:T(8,128)(2,1)}, bf16[768,1536]{1,0:T(8,128)(2,1)}, u32[]{:S(2)}, u32[]{:S(2)}) collective-permute-start(bf16[768,1536]{1,0:T(8,128)(2,1)} %wi_ref.3), channel_id=1, source_target_pairs={{0,1},{1,0},{2,3},{3,2},{4,5},{5,4},{6,7},{7,6},{8,9},{9,8},{10,11... | collective-permute-start | bytes 7077896 | tf_op jit(solution)/shard_map/ppermute | solution.py:25
  23.1 24.2 %collective-permute-start.6 = (f32[1,1536]{1,0:T(1,128)S(1)}, f32[1,1536]{1,0:T(1,128)S(1)}, u32[]{:S(2)}, u32[]{:S(2)}) collective-permute-start(f32[1,1536]{1,0:T(1,128)S(1)} %broadcast_in_dim.10.bi_ref), channel_id=1, source_target_pairs={{0,1},{1,0},{2,3},{3,2},{4,5},{5,4},{6,7},{7,6},{8,9},{9,8},{10,11... | collective-permute-start | bytes 18440 | tf_op jit(solution)/shard_map/ppermute | solution.py:25
  23.7 23.6 %collective-permute-start.8 = (bf16[512,768]{1,0:T(8,128)(2,1)}, bf16[512,768]{1,0:T(8,128)(2,1)S(1)}, u32[]{:S(2)}, u32[]{:S(2)}) collective-permute-start(bf16[512,768]{1,0:T(8,128)(2,1)} %get-tuple-element.133), channel_id=1, source_target_pairs={{0,2},{2,0},{4,6},{6,4},{8,10},{10,8},{12,14},{14,12},{16,18},{18,... | collective-permute-start | bytes 2359304 | tf_op jit(solution)/shard_map/ppermute | solution.py:25
  82.1 15.4 %collective-permute-start.10 = (bf16[8,48,768]{2,1,0:T(8,128)(2,1)S(1)}, bf16[8,48,768]{2,1,0:T(8,128)(2,1)S(1)}, u32[]{:S(2)}, u32[]{:S(2)}) collective-permute-start(bf16[8,48,768]{2,1,0:T(8,128)(2,1)S(1)} %get-tuple-element.139), channel_id=1, source_target_pairs={{0,2},{2,0},{4,6},{6,4},{8,10},{10,8},{12,14},{14,12},{16,18},{18,... | collective-permute-start | bytes 1769480 | tf_op jit(solution)/shard_map/ppermute | solution.py:25
  83.7 15.1 %collective-permute-start.11 = (bf16[8,48,768]{2,1,0:T(8,128)(2,1)S(1)}, bf16[8,48,768]{2,1,0:T(8,128)(2,1)S(1)}, u32[]{:S(2)}, u32[]{:S(2)}) collective-permute-start(bf16[8,48,768]{2,1,0:T(8,128)(2,1)S(1)} %get-tuple-element.140), channel_id=1, source_target_pairs={{0,4},{2,6},{4,0},{6,2},{8,12},{10,14},{12,8},{14,10},{16,20},{18,... | collective-permute-start | bytes 1769480 | tf_op jit(solution)/shard_map/ppermute | solution.py:25
  99.1 29.3 %collective-permute-start.13 = (bf16[2,768,768]{2,1,0:T(8,128)(2,1)S(1)}, bf16[2,768,768]{2,1,0:T(8,128)(2,1)S(1)}, u32[]{:S(2)}, u32[]{:S(2)}) collective-permute-start(bf16[2,768,768]{2,1,0:T(8,128)(2,1)S(1)} %get-tuple-element.162), channel_id=1, source_target_pairs={{0,1},{1,0},{2,3},{3,2},{4,5},{5,4},{6,7},{7,6},{8,9},{9,8},{10,11... | collective-permute-start | bytes 7077896 | tf_op jit(solution)/shard_map/ppermute | solution.py:25
  100.1 26.3 %collective-permute-start.12 = (bf16[512,768]{1,0:T(8,128)(2,1)S(1)}, bf16[512,768]{1,0:T(8,128)(2,1)S(1)}, u32[]{:S(2)}, u32[]{:S(2)}) collective-permute-start(bf16[512,768]{1,0:T(8,128)(2,1)S(1)} %get-tuple-element.151), channel_id=1, source_target_pairs={{0,2},{2,0},{4,6},{6,4},{8,10},{10,8},{12,14},{14,12},{16,18},{18,... | collective-permute-start | bytes 2359304 | tf_op jit(solution)/shard_map/ppermute | solution.py:25
  100.6 18.6 %collective-permute-start.14 = (bf16[4,48,768]{2,1,0:T(8,128)(2,1)S(1)}, bf16[4,48,768]{2,1,0:T(8,128)(2,1)S(1)}, u32[]{:S(2)}, u32[]{:S(2)}) collective-permute-start(bf16[4,48,768]{2,1,0:T(8,128)(2,1)S(1)} %get-tuple-element.149), channel_id=1, source_target_pairs={{0,4},{2,6},{4,0},{6,2},{8,12},{10,14},{12,8},{14,10},{16,20},{18,... | collective-permute-start | bytes 884744 | tf_op jit(solution)/shard_map/ppermute | solution.py:25
  102.2 24.2 %collective-permute-start.15 = (bf16[4,48,768]{2,1,0:T(8,128)(2,1)S(1)}, bf16[4,48,768]{2,1,0:T(8,128)(2,1)S(1)}, u32[]{:S(2)}, u32[]{:S(2)}) collective-permute-start(bf16[4,48,768]{2,1,0:T(8,128)(2,1)S(1)} %get-tuple-element.150), channel_id=1, source_target_pairs={{0,2},{2,0},{4,6},{6,4},{8,10},{10,8},{12,14},{14,12},{16,18},{18,... | collective-permute-start | bytes 884744 | tf_op jit(solution)/shard_map/ppermute | solution.py:25
  129.2 23.6 %collective-permute-start.19 = (bf16[2,96,768]{2,1,0:T(8,128)(2,1)S(1)}, bf16[2,96,768]{2,1,0:T(8,128)(2,1)S(1)}, u32[]{:S(2)}, u32[]{:S(2)}) collective-permute-start(bf16[2,96,768]{2,1,0:T(8,128)(2,1)S(1)} %get-tuple-element.169), channel_id=1, source_target_pairs={{0,8},{2,10},{4,12},{6,14},{8,0},{10,2},{12,4},{14,6},{16,24},{18,... | collective-permute-start | bytes 884744 | tf_op jit(solution)/shard_map/ppermute | solution.py:25
  130.9 22.0 %collective-permute-start.17 = (bf16[8,48,768]{2,1,0:T(8,128)(2,1)S(1)}, bf16[8,48,768]{2,1,0:T(8,128)(2,1)S(1)}, u32[]{:S(2)}, u32[]{:S(2)}) collective-permute-start(bf16[8,48,768]{2,1,0:T(8,128)(2,1)S(1)} %get-tuple-element.167), channel_id=1, source_target_pairs={{0,2},{2,0},{4,6},{6,4},{8,10},{10,8},{12,14},{14,12},{16,18},{18,... | collective-permute-start | bytes 1769480 | tf_op jit(solution)/shard_map/ppermute | solution.py:25
  131.4 21.5 %collective-permute-start.18 = (bf16[8,72,768]{2,1,0:T(8,128)(2,1)S(1)}, bf16[8,72,768]{2,1,0:T(8,128)(2,1)S(1)}, u32[]{:S(2)}, u32[]{:S(2)}) collective-permute-start(bf16[8,72,768]{2,1,0:T(8,128)(2,1)S(1)} %get-tuple-element.168), channel_id=1, source_target_pairs={{0,4},{2,6},{4,0},{6,2},{8,12},{10,14},{12,8},{14,10},{16,20},{18,... | collective-permute-start | bytes 2654216 | tf_op jit(solution)/shard_map/ppermute | solution.py:25
  153.3 15.9 %collective-permute-start.21 = (bf16[2,768,384]{2,1,0:T(8,128)(2,1)S(1)}, bf16[2,768,384]{2,1,0:T(8,128)(2,1)S(1)}, u32[]{:S(2)}, u32[]{:S(2)}) collective-permute-start(bf16[2,768,384]{2,1,0:T(8,128)(2,1)S(1)} %get-tuple-element.188), channel_id=1, source_target_pairs={{0,1},{1,0},{2,3},{3,2},{4,5},{5,4},{6,7},{7,6},{8,9},{9,8},{10,11... | collective-permute-start | bytes 3538952 | tf_op jit(solution)/shard_map/ppermute | solution.py:25
  153.4 15.5 %collective-permute-start.24 = (bf16[1,96,768]{2,1,0:T(8,128)(2,1)S(1)}, bf16[1,96,768]{2,1,0:T(8,128)(2,1)S(1)}, u32[]{:S(2)}, u32[]{:S(2)}) collective-permute-start(bf16[1,96,768]{2,1,0:T(8,128)(2,1)S(1)} %get-tuple-element.180), channel_id=1, source_target_pairs={{0,16},{2,18},{4,20},{6,22},{8,24},{10,26},{12,28},{14,30},{16,0},... | collective-permute-start | bytes 442376 | tf_op jit(solution)/shard_map/ppermute | solution.py:25
  156.0 12.9 %collective-permute-start.22 = (bf16[4,48,768]{2,1,0:T(8,128)(2,1)S(1)}, bf16[4,48,768]{2,1,0:T(8,128)(2,1)S(1)}, u32[]{:S(2)}, u32[]{:S(2)}) collective-permute-start(bf16[4,48,768]{2,1,0:T(8,128)(2,1)S(1)} %get-tuple-element.178), channel_id=1, source_target_pairs={{0,4},{2,6},{4,0},{6,2},{8,12},{10,14},{12,8},{14,10},{16,20},{18,... | collective-permute-start | bytes 884744 | tf_op jit(solution)/shard_map/ppermute | solution.py:25
  169.8 12.9 %collective-permute-start.28 = (bf16[1,96,768]{2,1,0:T(8,128)(2,1)S(1)}, bf16[1,96,768]{2,1,0:T(8,128)(2,1)S(1)}, u32[]{:S(2)}, u32[]{:S(2)}) collective-permute-start(bf16[1,96,768]{2,1,0:T(8,128)(2,1)S(1)} %get-tuple-element.195.refs_6_), channel_id=1, source_target_pairs={{0,16},{2,18},{4,20},{6,22},{8,24},{10,26},{12,28},{14,30},{16,0},... | collective-permute-start | bytes 442376 | tf_op jit(solution)/shard_map/ppermute | solution.py:25
  170.2 13.7 %collective-permute-start.27 = (bf16[2,120,768]{2,1,0:T(8,128)(2,1)S(1)}, bf16[2,120,768]{2,1,0:T(8,128)(2,1)S(1)}, u32[]{:S(2)}, u32[]{:S(2)}) collective-permute-start(bf16[2,120,768]{2,1,0:T(8,128)(2,1)S(1)} %get-tuple-element.194), channel_id=1, source_target_pairs={{0,8},{2,10},{4,12},{6,14},{8,0},{10,2},{12,4},{14,6},{16,24},{18,... | collective-permute-start | bytes 1105928 | tf_op jit(solution)/shard_map/ppermute | solution.py:25
  170.6 13.3 %collective-permute-start.26 = (bf16[8,64,384]{2,1,0:T(8,128)(2,1)S(1)}, bf16[8,64,384]{2,1,0:T(8,128)(2,1)S(1)}, u32[]{:S(2)}, u32[]{:S(2)}) collective-permute-start(bf16[8,64,384]{2,1,0:T(8,128)(2,1)S(1)} %get-tuple-element.193), channel_id=1, source_target_pairs={{0,4},{2,6},{4,0},{6,2},{8,12},{10,14},{12,8},{14,10},{16,20},{18,... | collective-permute-start | bytes 1179656 | tf_op jit(solution)/shard_map/ppermute | solution.py:25
  171.5 12.6 %collective-permute-start.25 = (bf16[8,80,384]{2,1,0:T(8,128)(2,1)S(1)}, bf16[8,80,384]{2,1,0:T(8,128)(2,1)S(1)}, u32[]{:S(2)}, u32[]{:S(2)}) collective-permute-start(bf16[8,80,384]{2,1,0:T(8,128)(2,1)S(1)} %get-tuple-element.192), channel_id=1, source_target_pairs={{0,2},{2,0},{4,6},{6,4},{8,10},{10,8},{12,14},{14,12},{16,18},{18,... | collective-permute-start | bytes 1474568 | tf_op jit(solution)/shard_map/ppermute | solution.py:25
  185.6 13.9 %collective-permute-start.33 = (bf16[2,96,768]{2,1,0:T(8,128)(2,1)S(1)}, bf16[2,96,768]{2,1,0:T(8,128)(2,1)S(1)}, u32[]{:S(2)}, u32[]{:S(2)}) collective-permute-start(bf16[2,96,768]{2,1,0:T(8,128)(2,1)S(1)} %get-tuple-element.212.refs_6_), channel_id=1, source_target_pairs={{0,8},{2,10},{4,12},{6,14},{8,0},{10,2},{12,4},{14,6},{16,24},{18,... | collective-permute-start | bytes 884744 | tf_op jit(solution)/shard_map/ppermute | solution.py:25
  215.7 12.8 %collective-permute-start.42 = (bf16[8,48,768]{2,1,0:T(8,128)(2,1)S(1)}, bf16[8,48,768]{2,1,0:T(8,128)(2,1)S(1)}, u32[]{:S(2)}, u32[]{:S(2)}) collective-permute-start(bf16[8,48,768]{2,1,0:T(8,128)(2,1)S(1)} %get-tuple-element.227.refs_6_), channel_id=1, source_target_pairs={{0,2},{2,0},{4,6},{6,4},{8,10},{10,8},{12,14},{14,12},{16,18},{18,... | collective-permute-start | bytes 1769480 | tf_op jit(solution)/shard_map/ppermute | solution.py:25
  241.5 17.1 %collective-permute-start.49 = (bf16[8,72,768]{2,1,0:T(8,128)(2,1)S(1)}, bf16[8,72,768]{2,1,0:T(8,128)(2,1)S(1)}, u32[]{:S(2)}, u32[]{:S(2)}) collective-permute-start(bf16[8,72,768]{2,1,0:T(8,128)(2,1)S(1)} %get-tuple-element.234.refs_3_), channel_id=1, source_target_pairs={{0,4},{2,6},{4,0},{6,2},{8,12},{10,14},{12,8},{14,10},{16,20},{18,... | collective-permute-start | bytes 2654216 | tf_op jit(solution)/shard_map/ppermute | solution.py:25
  (48 other events, 368.9 us)
where the time goes:
time: 290 us; the launch traced here: 285 us
  Pallas kernels  131 us (45%)
  waiting for transfers between devices  78 us (27%)
  starting transfers between devices  57.4 us (20%)
  local copies, waits for them, and re-layouts  8.51 us (3%)
  other arithmetic  8.41 us (3%)
    ppermute x54, waiting for transfers between devices, swap_bit(): lax.ppermute(x, axis, [(i, i ^ 1 << bit) for i in range(lax.axis_size(axi...  78 us
    ppermute x54, starting transfers between devices, swap_bit(): lax.ppermute(x, axis, [(i, i ^ 1 << bit) for i in range(lax.axis_size(axi...  57.4 us
    pallas_call x2, Pallas kernels, attention_back(): pl.pallas_call(functools.partial(attend_back_kernel, ends), grid=(pairs,)...  30.2 us
    pallas_call x1, Pallas kernels, ffn(): pl.pallas_call(functools.partial(ffn_kernel, tiles), grid=(tiles + per,),...  29.7 us
    pallas_call x2, Pallas kernels, ffn_back(): pl.pallas_call(functools.partial(ffn_back_kernel, last), grid=(tiles,), i...  26 us
    pallas_call x1, Pallas kernels, attention(): pl.pallas_call(functools.partial(attend_kernel, pairs), grid=(pairs,), in...  21.8 us
    pallas_call x13, Pallas kernels, advance(): pl.pallas_call(kernel, in_specs=[pl.BlockSpec(memory_space=pltpu.SMEM)] +...  11.7 us
    pallas_call x1, Pallas kernels, input_gradient(): pl.pallas_call(input_kernel, grid=(pairs,), in_specs=[pl.BlockSpec(part,...  8.74 us
  transfers between devices with their start and end apart: 54, of which 26 were waited for; matrix products, arithmetic and copies ran while one was open for 5% of the time, Pallas kernels for 32%

commit v1 on v0

--- a/solution.py
+++ b/solution.py
@@ -188,7 +188,8 @@
 
 def ffn_kernel(
     tiles, mid_n_ref, par_ref, wi_ref, mi_ref, bi_ref, mbi_ref, wd_ref, md_ref, ca_ref, cb_ref, wt_ref,
-    act_t_ref, slope_ref, h1_t_ref, out_ref, ds2_ref, df_ref, vec_ref, gm_ref, h1_low, acc, act_m,
+    act_t_ref, slope_ref, h1_t_ref, kept_ref, first_ref, rest_ref, ds2_ref, df_ref, vec_ref, gm_ref,
+    h1_low, acc, act_m,
 ):
     step = pl.program_id(0)
     own = step < tiles // 2
@@ -235,7 +236,11 @@
         for at in range(0, 2 * BLOCK, size):
             rows = slice(at, at + size)
             normed, rate = normalize(acc[rows, :])
-            out_ref[rows, :] = (normed * gain + par_ref[4:5, :]).astype(BF16)
+            out = (normed * gain + par_ref[4:5, :]).astype(BF16)
+            if at < BLOCK:
+                kept_ref[rows, :] = out
+            else:
+                (first_ref if at == BLOCK else rest_ref)[...] = out
             cot_ref, first = (ca_ref, at) if at < BLOCK else (cb_ref, at - BLOCK)
             d_y = cot_ref[first : first + size, :].astype(F32) * wt_ref[rows, :]
             d_s2 = norm_back(d_y, normed, rate, gain)
@@ -282,7 +287,9 @@
             pl.BlockSpec((TILE, rows), lambda j: (own_at(j), 0)),
             pl.BlockSpec((rows, TILE), lambda j: (0, jnp.minimum(j, tiles - 1))),
             whole((width, rows)),
-            whole((rows, width)),
+            whole((BLOCK, width)),
+            whole((BLOCK // 2, width)),
+            whole((BLOCK // 2, width)),
             whole((rows, width)),
             whole((rows, width)),
             whole((8, width)),
@@ -292,7 +299,9 @@
             jax.ShapeDtypeStruct((hidden // 2, rows), BF16),
             pltpu.HBM((rows, hidden), BF16),
             jax.ShapeDtypeStruct((width, rows), BF16),
-            jax.ShapeDtypeStruct((rows, width), BF16),
+            jax.ShapeDtypeStruct((BLOCK, width), BF16),
+            jax.ShapeDtypeStruct((BLOCK // 2, width), BF16),
+            jax.ShapeDtypeStruct((BLOCK // 2, width), BF16),
             jax.ShapeDtypeStruct((rows, width), F32),
             jax.ShapeDtypeStruct((rows, width), BF16),
             jax.ShapeDtypeStruct((8, width), F32),
@@ -647,6 +656,7 @@
         self.left = [list(reversed(range(bits)))] * 2
         self.job = 0
         self.alone = alone
+        self.keep = pltpu.VMEM
         self.extra, self.finish = extra, finish
         units = [0] * len(own)
         for stream in streams:
@@ -680,7 +690,7 @@
             bits = self.there[job]
             together = bits[0] == bits[1]
             half = self.shapes(1 << (len(left[0]) - 1), together)
-            shapes = [pltpu.VMEM(x.shape, x.dtype) for x in half] + half
+            shapes = [self.keep(x.shape, x.dtype) for x in half] + half
             self.left = [[b for b in mine if b != bit] for mine, bit in zip(left, bits)]
         else:
             bits = None
@@ -904,7 +914,7 @@
         w_output, mate_out,
     )
     cot_got = swap_bit(after(cot_given, x_got), "tok", 0)
-    act_t, slope, h1_t, out, d_s2, d_f, end_vec, g_mate = ffn(
+    act_t, slope, h1_t, out_kept, out_first, out_rest, d_s2, d_f, end_vec, g_mate = ffn(
         mid_n, params, w_inner, mate_in, own_bias, mate_bias, w_outer, mate_down,
         (cot_kept, cot_got), weight,
     )
@@ -929,13 +939,20 @@
 
         def write(outs, stream, spot, value):
             value = value.astype(F32)
-            outs[0][spot, :, stream * width : (stream + 1) * width] = value[: rows[0]]
-            if stream == 1:
-                outs[1][spot] = value[rows[0] :]
+            one = width // size
+            outs[0][spot, :, stream * width : (stream + 1) * width] = value[:one]
+            more = rows[stream] - one - 8
+            first = spot * more + (third if stream else 0)
+            outs[1][first : first + more, :] = value[one : one + more]
+            if stream == 0 and spot == 0:
+                outs[2][...] = value[one + more :]
+            else:
+                outs[2][...] += value[one + more :]
 
         return [
-            jax.ShapeDtypeStruct((size, rows[0], 2 * width), F32),
-            jax.ShapeDtypeStruct((size, rows[1] - rows[0], width), F32),
+            jax.ShapeDtypeStruct((size, width // size, 2 * width), F32),
+            jax.ShapeDtypeStruct((rest, width), F32),
+            jax.ShapeDtypeStruct((8, width), F32),
         ], write
 
     size = lax.axis_size("tok")
@@ -951,39 +968,25 @@
         1, after(d_f, sent), slope, mate_in, mate_down, h1_t, d_s2
     )
     sent = advance([down], gi_mate)
-    out_got = swap_bit(after(out[BLOCK:], sent), "tok", 0)
+    first_got = swap_bit(after(out_first, sent), "tok", 0)
     got_in = mate(after(gi_mate, sent))
     gi_own, gb_own, go_own, go_mate, d_s1, d_a, mid_vec = ffn_back(
         0, after(d_f, sent), slope, w_inner, w_outer, h1_t, d_h1, mid_n, mid_rate, ctx_t, params
     )
-    got_out = mate(after(go_mate, down.inputs[-2:], out_got) if fits else go_mate)
+    got_out = mate(after(go_mate, down.inputs[-2:], first_got) if fits else go_mate)
+    third = 8 * size
     inner = Sum(
-        [[(0, 0, width)], [(0, width, width), (1, 0, rest)]],
+        [[(0, 0, width), (1, 0, third)], [(0, width, width), (1, third, rest - third)]],
         [gi_own, go_own], [got_in, got_out], finish=finish_inner, alone=False,
     )
     sent = advance([inner, down], gi_own)
+    rest_got = swap_bit(after(out_rest, sent), "tok", 0)
     gw_mate, gw_mates, gw_own, dp_early = attention_back(
         (1, pairs, pairs + 1), lambda p: jnp.where(p < pairs, p + pairs, 0), swap_lanes, qkv, ctx_t,
         lse, (w_output, mate_out), after(d_a, sent), x_t,
     )
-    sent = advance([inner, down], gw_own)
+    sent = advance([inner, down], gw_own, rest_got)
     gw_got, gw_gots = (mate(x) for x in after((gw_mate, gw_mates), sent))
-
-    gb_own, gb_mate = gb_own.reshape(-1, width), gb_mate.reshape(-1, width)
-    own_rows = gb_own.shape[0]
-    small = jnp.concatenate([end_vec[:3], mid_vec[:2], gb_own, gb_mate], axis=0)
-    theirs = mate(small)
-    small = jnp.concatenate(
-        [
-            small[:5] + theirs[:5],
-            small[5 : 5 + own_rows] + theirs[5 + own_rows :],
-            jnp.zeros((1, width), F32),
-        ],
-        axis=0,
-    )
-    high = small.astype(BF16)
-    low = (small - high.astype(F32)).astype(BF16)
-    high, low = side_by_side(high), side_by_side(low)
 
     gw_owns, dp_late = attention_back(
         (pairs - 1,), lambda p: p + 1, swap_lanes, qkv, ctx_t, lse, (w_output,), after(d_a, sent), x_t
@@ -993,8 +996,7 @@
     def finish_last(rows):
         def write(outs, stream, spot, value):
             value = value.astype(F32)
-            extra = high.shape[0]
-            count = rows[stream] - extra
+            count = rows[stream]
             pieces = [(0, spot * count + width + head, count)]
             if stream == 0:
                 one = width // size
@@ -1008,26 +1010,41 @@
                             done : done + step, at * LANES : (at + 1) * LANES
                         ]
                     done, first, length = done + step, first + step, length - step
-            if stream == 0 and spot == 0:
-                outs[3][...] = value[count:]
-            else:
-                outs[3][...] += value[count:]
-
-        return [jax.ShapeDtypeStruct((width, pairs * LANES), F32)] * 3 + [
-            jax.ShapeDtypeStruct(high.shape, F32)
-        ], write
+
+        return [jax.ShapeDtypeStruct((width, pairs * LANES), F32)] * 3, write
 
     rows = (pairs - 1) * width
     last = Sum(
         [[(0, 0, width), (1, 0, head)], [(1, head, rows - head)]],
         [x.reshape(-1, 3 * LANES) for x in (gw_own, gw_owns)],
         [x.reshape(-1, 3 * LANES) for x in (gw_got, gw_gots)],
-        extra=(high, low), finish=finish_last,
-    )
+        finish=finish_last,
+    )
+    for one in (last, inner, down):
+        one.keep = pltpu.VMEM
     sent = advance([last, inner, down], gw_owns)
-    out = joined(out[:BLOCK], out_got, half)
+    out = joined(out_kept, jnp.concatenate([first_got, rest_got], axis=0), half)
+    own_rows = gb_own.size // width
+
+    def small_vectors(sent):
+        end, mid, own, other = after((end_vec, mid_vec, gb_own, gb_mate), sent)
+        own, other = own.reshape(-1, width), other.reshape(-1, width)
+        small = jnp.concatenate([end[:3], mid[:2], own, other], axis=0)
+        theirs = mate(small)
+        small = jnp.concatenate(
+            [
+                small[:5] + theirs[:5],
+                small[5 : 5 + own_rows] + theirs[5 + own_rows :],
+                jnp.zeros((1, width), F32),
+            ],
+            axis=0,
+        )
+        high = small.astype(BF16)
+        low = (small - high.astype(F32)).astype(BF16)
+        return small, (high, low)
+
     dx_kept, dx_given = input_gradient(dp_early, after(dp_late, sent), own_w, mate_w, d_s1)
-    dx_got = []
+    dx_got, finals = [], []
     if fits:
         while last.job <= 2 * len(last.there):
             for one in (inner, down):
@@ -1040,22 +1057,28 @@
                 part = dx_given[first : first + BLOCK // 2]
                 others = [swap_bit(after(part, last.inputs[0]), "tok", 0)]
                 dx_got += others
-            advance(sums, *others)
-        g_down, (g_in, g_out), (g_query, g_key, g_value, sums) = (
+            ending = [one for one in sums if one is not last and one.job == 2 * len(one.there)]
+            sent = advance([one for one in sums if one not in ending], *others, *finals)
+            if last.job == 2:
+                small, inner.extra = small_vectors(sent)
+            finals = []
+            for one in ending:
+                advance([one], sent)
+                finals += one.found
+        g_down, (g_in, g_out, small), (g_query, g_key, g_value) = (
             down.found[0], inner.found, last.found
         )
-        small = jnp.concatenate([sums[: small.shape[0]], sums[small.shape[0] :]], axis=1)
     else:
         dx_got = [swap_bit(dx_given, "tok", 0)]
         g_down = jnp.concatenate([down.found[0][0], down.found[1][0]], axis=0)
         g_in = jnp.concatenate([inner.found[0][0], inner.found[1][0]], axis=1)
-        g_out = inner.found[1][1]
+        g_out = jnp.concatenate([inner.found[0][1], inner.found[1][1]], axis=0)
         whole_w = jnp.concatenate(last.found[0] + last.found[1], axis=0)
         whole_w = whole_w.reshape(pairs, width, 3, LANES)
         g_query, g_key, g_value = (
             jnp.concatenate([whole_w[p, :, at] for p in range(pairs)], axis=1) for at in range(3)
         )
-        small = lax.psum(small, "tok")
+        small = lax.psum(small_vectors(())[0], "tok")
     dx_got = jnp.concatenate(dx_got, axis=0).astype(F32)
     grad_tokens = joined(dx_kept, dx_got, half)
     g_down = g_down.reshape(hidden, width)

time: 290 us -> 287 us (0.990)
  starting transfers between devices: 57.4 us -> 45.6 us
  waiting for transfers between devices: 78 us -> 85.7 us
  Pallas kernels: 131 us -> 135 us
  other arithmetic: 8.41 us -> 5.1 us
    ppermute x54 -> x55, starting transfers between devices: 57.4 us -> 45.6 us  [swap_bit(): lax.ppermute(x, axis, [(i, i ^ 1 << bit) for i in range(lax.axis_size(axi...]
    ppermute x54 -> x55, waiting for transfers between devices: 78 us -> 85.7 us  [swap_bit(): lax.ppermute(x, axis, [(i, i ^ 1 << bit) for i in range(lax.axis_size(axi...]
    pallas_call x13 -> x15, Pallas kernels: 11.7 us -> 15.6 us  [advance(): pl.pallas_call(kernel, in_specs=[pl.BlockSpec(memory_space=pltpu.SMEM)] +...]
  transfers between devices with their start and end apart: 54 -> 55, of which waited for: 26 -> 23; matrix products, arithmetic and copies ran while one was open for 5% -> 4% of each run, Pallas kernels for 32% -> 35%
where the time goes in v1:
time: 287 us; the launch traced here: 282 us
  Pallas kernels  135 us (47%)
  waiting for transfers between devices  85.7 us (30%)
  starting transfers between devices  45.6 us (16%)
  local copies, waits for them, and re-layouts  8.64 us (3%)
  other arithmetic  5.1 us (2%)
    ppermute x55, waiting for transfers between devices, swap_bit(): lax.ppermute(x, axis, [(i, i ^ 1 << bit) for i in range(lax.axis_size(axi...  85.7 us
    ppermute x55, starting transfers between devices, swap_bit(): lax.ppermute(x, axis, [(i, i ^ 1 << bit) for i in range(lax.axis_size(axi...  45.6 us
    pallas_call x2, Pallas kernels, attention_back(): pl.pallas_call(functools.partial(attend_back_kernel, ends), grid=(pairs,)...  30.2 us
    pallas_call x1, Pallas kernels, ffn(): pl.pallas_call(functools.partial(ffn_kernel, tiles), grid=(tiles + per,),...  29.9 us
    pallas_call x2, Pallas kernels, ffn_back(): pl.pallas_call(functools.partial(ffn_back_kernel, last), grid=(tiles,), i...  25.9 us
    pallas_call x1, Pallas kernels, attention(): pl.pallas_call(functools.partial(attend_kernel, pairs), grid=(pairs,), in...  21.8 us
    pallas_call x15, Pallas kernels, advance(): pl.pallas_call(kernel, in_specs=[pl.BlockSpec(memory_space=pltpu.SMEM)] +...  15.6 us
    pallas_call x1, Pallas kernels, input_gradient(): pl.pallas_call(input_kernel, grid=(pairs,), in_specs=[pl.BlockSpec(part,...  8.81 us
  transfers between devices with their start and end apart: 55, of which 23 were waited for; matrix products, arithmetic and copies ran while one was open for 4% of the time, Pallas kernels for 35%

profile of v1, /device:TPU:0, one launch (start us, length us, event | category | flops | bytes accessed | tf_op | source)
XLA Modules:
  0.0 281.8 jit_solution(1141466126983795734)
XLA Ops:
  2.3 3.0 %collective-permute-start = (bf16[512,768]{1,0:T(8,128)(2,1)S(1)}, bf16[512,768]{1,0:T(8,128)(2,1)S(1)}, u32[]{:S(2)}, u32[]{:S(2)}) collective-permute-start(bf16[512,768]{1,0:T(8,128)(2,1)S(1)} %get-tuple-element.275), channel_id=1, source_target_pairs={{0,2},{2,0},{4,6},{6,4},{8,10},{10,8},{12,14},{14,12},{16,18},{18,... | collective-permute-start | bytes 2359304 | tf_op jit(solution)/shard_map/ppermute | solution.py:25
  7.1 2.4 constant_dynamic-slice_fusion
  11.0 5.4 %collective-permute-done.1.mq_ref = bf16[768,384]{1,0:T(8,128)(2,1)S(1)} collective-permute-done((bf16[768,384]{1,0:T(8,128)(2,1)}, bf16[768,384]{1,0:T(8,128)(2,1)S(1)}, u32[]{:S(2)}, u32[]{:S(2)}) %collective-permute-start.1) | collective-permute-done | bytes 589856 | tf_op jit(solution)/shard_map/ppermute | solution.py:25
  16.6 6.2 %collective-permute-done.xb_ref = bf16[512,768]{1,0:T(8,128)(2,1)S(1)} collective-permute-done((bf16[512,768]{1,0:T(8,128)(2,1)S(1)}, bf16[512,768]{1,0:T(8,128)(2,1)S(1)}, u32[]{:S(2)}, u32[]{:S(2)}) %collective-permute-start) | collective-permute-done | bytes 786464 | tf_op jit(solution)/shard_map/ppermute | solution.py:25
  25.4 21.8 %attention_forward.1 = (bf16[1024,2304]{1,0:T(8,128)(2,1)}, f32[6,2,1024]{2,1,0:T(2,128)S(1)}, bf16[768,1024]{1,0:T(8,128)(2,1)}, bf16[768,1024]{1,0:T(8,128)(2,...) custom-call(s32[1,768]{1,0:T(1,128)S(1)} %broadcast_in_dim_reshape.3.swap_ref, ...), custom_call_target="tpu_custom_call" | custom-call | flops 11274289152 | bytes 18874368 | tf_op jit(solution)/shard_map/attention_forward/pallas_call | solution.py:154
  47.3 29.9 %feed_forward.1 = (bf16[1536,1024]{1,0:T(8,128)(2,1)S(1)}, bf16[1024,3072]{1,0:T(8,128)(2,1)}, bf16[768,1024]{1,0:T(8,128)(2,1)S(1)}, bf16[512,768]{1,0:T(8,128)...) custom-call(f32[1024,768]{1,0:T(8,128)} %get-tuple-element.141.mid_n, ...), custom_call_target="tpu_custom_call" | custom-call | flops 9663676416 | bytes 34603008 | tf_op jit(solution)/shard_map/feed_forward/pallas_call | solution.py:270
  77.3 3.0 %weight_gradient.1 = bf16[1536,768]{1,0:T(8,128)(2,1)S(1)} custom-call(bf16[1536,1024]{1,0:T(8,128)(2,1)S(1)} %get-tuple-element.147.a_ref, bf16[1024,768]{1,0:T(8,128)(2,1)S(1)} %get-tuple-element.164.b_ref.df_ref), custom_call_target="tpu_custom_call" | custom-call | flops 2415919104 | bytes 7077888 | tf_op jit(solution)/shard_map/weight_gradient/pallas_call | solution.py:333
  85.5 10.4 %feed_forward_back.2 = (bf16[2,768,768]{2,1,0:T(8,128)(2,1)S(1)}, f32[1,1536]{1,0:T(1,128)S(1)}, f32[1024,768]{1,0:T(8,128)S(1)}) custom-call(bf16[1024,768]{1,0:T(8,128)(2,1)S(1)} %get-tuple-element.164.b_ref.df_ref, bf16[1024,3072]{1,0:T(8,128)(2,1)} %get-tuple-element.153.slope_ref, bf16[768,1536]{1,0:T(8,128)(2,1)} %collective-permute-done.5.mi_ref.wi_ref, ...), custom_call_target="tpu_custom_call" | custom-call | flops 7247757312 | bytes 24379392 | tf_op jit(solution)/shard_map/feed_forward_back/pallas_call | solution.py:422
  103.0 15.4 %feed_forward_back.3 = (bf16[2,768,768]{2,1,0:T(8,128)(2,1)S(1)}, f32[1,1536]{1,0:T(1,128)S(1)}, bf16[384,768]{1,0:T(8,128)(2,1)S(1)}, bf16[384,768]{1,0:T(8,128...) custom-call(bf16[1024,768]{1,0:T(8,128)(2,1)S(1)} %get-tuple-element.164.b_ref.df_ref, ...), custom_call_target="tpu_custom_call" | custom-call | flops 7247757312 | bytes 24379392 | tf_op jit(solution)/shard_map/feed_forward_back/pallas_call | solution.py:422
  125.6 19.9 %attention_backward.2 = (bf16[1,768,384]{2,1,0:T(8,128)(2,1)S(1)}, bf16[2,768,384]{2,1,0:T(8,128)(2,1)S(1)}, bf16[1,768,384]{2,1,0:T(8,128)(2,1)S(1)}, bf16[1024,1536]{1,0:T(8,128)(2,1)}) custom-call(s32[1,768]{1,0:T(1,128)S(1)} %broadcast_in_dim_reshape.3.swap_ref, bf16[1024,2304]{1,0:T(8,128)(2,1)} %get-tuple-element.180.qkv_ref, ...), custom_call_target="tpu_custom_call" | custom-call | flops 13958643712 | bytes 11010048 | tf_op jit(solution)/shard_map/attention_backward/pallas_call | solution.py:533
  145.5 3.2 %collective-permute-done.17 = bf16[256,768]{1,0:T(8,128)(2,1)S(1)} collective-permute-done((bf16[256,768]{1,0:T(8,128)(2,1)S(1)}, bf16[256,768]{1,0:T(8,128)(2,1)S(1)}, u32[]{:S(2)}, u32[]{:S(2)}) %collective-permute-start.17) | collective-permute-done | bytes 393248 | tf_op jit(solution)/shard_map/ppermute | solution.py:25
  149.2 2.7 collective-permute-start.25
  152.9 10.2 %attention_backward.3 = (bf16[2,768,384]{2,1,0:T(8,128)(2,1)S(1)}, bf16[1024,768]{1,0:T(8,128)(2,1)}) custom-call(s32[1,768]{1,0:T(1,128)S(1)} %broadcast_in_dim_reshape.3.swap_ref, bf16[1024,2304]{1,0:T(8,128)(2,1)} %get-tuple-element.180.qkv_ref, bf16[768,1024]{1,0:T(8,128)(2,1)} %get-tuple-element.167.refs_2_.ctx_t_ref, ...), custom_call_target="tpu_custom_call" | custom-call | flops 6979321856 | bytes 11010048 | tf_op jit(solution)/shard_map/attention_backward/pallas_call | solution.py:533
  167.7 8.8 %input_gradient.1 = (f32[512,768]{1,0:T(8,128)S(1)}, bf16[512,768]{1,0:T(8,128)(2,1)S(1)}) custom-call(bf16[1024,1536]{1,0:T(8,128)(2,1)} %get-tuple-element.185.first_ref.mate_ref, bf16[1024,768]{1,0:T(8,128)(2,1)} %get-tuple-element.209.later_ref, bf16[1024,1536]{1,0:T(8,128)(2,1)} %get-tuple-element.185.first_ref.mate_ref, bf16[768,384]{1,0:T(8,128)(2,1)} %wq_ref.3, ...), custom_call_target="tpu_custom_call" | custom-call | flops 3623878656 | bytes 11010048 | tf_op jit(solution)/shard_map/input_gradient/pallas_call | solution.py:586
  186.5 12.8 %collective-permute-done.30 = bf16[256,768]{1,0:T(8,128)(2,1)S(1)} collective-permute-done((bf16[256,768]{1,0:T(8,128)(2,1)S(1)}, bf16[256,768]{1,0:T(8,128)(2,1)S(1)}, u32[]{:S(2)}, u32[]{:S(2)}) %collective-permute-start.30) | collective-permute-done | bytes 393248 | tf_op jit(solution)/shard_map/ppermute | solution.py:25
  204.8 7.6 %collective-permute-done.36 = bf16[256,768]{1,0:T(8,128)(2,1)S(1)} collective-permute-done((bf16[256,768]{1,0:T(8,128)(2,1)S(1)}, bf16[256,768]{1,0:T(8,128)(2,1)S(1)}, u32[]{:S(2)}, u32[]{:S(2)}) %collective-permute-start.36) | collective-permute-done | bytes 393248 | tf_op jit(solution)/shard_map/ppermute | solution.py:25
  213.2 3.8 %collective-permute-done.40.refs_7_ = bf16[4,48,768]{2,1,0:T(8,128)(2,1)S(1)} collective-permute-done((bf16[4,48,768]{2,1,0:T(8,128)(2,1)S(1)}, bf16[4,48,768]{2,1,0:T(8,128)(2,1)S(1)}, u32[]{:S(2)}, u32[]{:S(2)}) %collective-permute-start.40) | collective-permute-done | bytes 294944 | tf_op jit(solution)/shard_map/ppermute | solution.py:25
  220.0 7.5 %collective-permute-done.41.refs_1_ = bf16[1,144,384]{2,1,0:T(8,128)(2,1)S(1)} collective-permute-done((bf16[1,144,384]{2,1,0:T(8,128)(2,1)S(1)}, bf16[1,144,384]{2,1,0:T(8,128)(2,1)S(1)}, u32[]{:S(2)}, u32[]{:S(2)}) %collective-permute-start.41) | collective-permute-done | bytes 110624 | tf_op jit(solution)/shard_map/ppermute | solution.py:25
  232.1 2.5 sum_step.24
  234.6 3.1 %collective-permute-done.45.refs_1_ = bf16[1,144,384]{2,1,0:T(8,128)(2,1)S(1)} collective-permute-done((bf16[1,144,384]{2,1,0:T(8,128)(2,1)S(1)}, bf16[1,144,384]{2,1,0:T(8,128)(2,1)S(1)}, u32[]{:S(2)}, u32[]{:S(2)}) %collective-permute-start.45) | collective-permute-done | bytes 110624 | tf_op jit(solution)/shard_map/ppermute | solution.py:25
  244.4 4.3 %collective-permute-done.48.refs_1_ = bf16[2,144,384]{2,1,0:T(8,128)(2,1)S(1)} collective-permute-done((bf16[2,144,384]{2,1,0:T(8,128)(2,1)S(1)}, bf16[2,144,384]{2,1,0:T(8,128)(2,1)S(1)}, u32[]{:S(2)}, u32[]{:S(2)}) %collective-permute-start.48) | collective-permute-done | bytes 221216 | tf_op jit(solution)/shard_map/ppermute | solution.py:25
  252.3 9.0 %collective-permute-done.49.refs_2_ = bf16[8,64,768]{2,1,0:T(8,128)(2,1)} collective-permute-done((bf16[8,64,768]{2,1,0:T(8,128)(2,1)}, bf16[8,64,768]{2,1,0:T(8,128)(2,1)}, u32[]{:S(2)}, u32[]{:S(2)}) %collective-permute-start.49) | collective-permute-done | bytes 786464 | tf_op jit(solution)/shard_map/ppermute | solution.py:25
  263.4 4.5 %sum_step.27 = (f32[16,48,1536]{2,1,0:T(8,128)}, f32[384,768]{1,0:T(8,128)}, f32[8,768]{1,0:T(8,128)S(1)}) custom-call(s32[1]{0:T(128)} %bitcast.3.place_ref, bf16[8,64,768]{2,1,0:T(8,128)(2,1)} %get-tuple-element.255.refs_0_, bf16[8,72,768]{2,1,0:T(8,128)(2,1)S(1)} %get-tuple-element.256.refs_1_, bf16[8,64,768]{2,1,0:T(8,128)(2,1)} %collective-permute-done.49.refs_2_, ...), custom_call_target="tpu_custom_call" | custom-call | flops 6303744 | bytes 6303744 | tf_op jit(solution)/shard_map/sum_step/pallas_call | solution.py:836
  275.6 4.0 %collective-permute-done.54.refs_3_ = bf16[8,64,384]{2,1,0:T(8,128)(2,1)S(1)} collective-permute-done((bf16[8,64,384]{2,1,0:T(8,128)(2,1)S(1)}, bf16[8,64,384]{2,1,0:T(8,128)(2,1)S(1)}, u32[]{:S(2)}, u32[]{:S(2)}) %collective-permute-start.54) | collective-permute-done | bytes 393248 | tf_op jit(solution)/shard_map/ppermute | solution.py:25
  (198 shorter events, 78.7 us)
Async XLA Ops:
  2.3 20.5 %collective-permute-start = (bf16[512,768]{1,0:T(8,128)(2,1)S(1)}, bf16[512,768]{1,0:T(8,128)(2,1)S(1)}, u32[]{:S(2)}, u32[]{:S(2)}) collective-permute-start(bf16[512,768]{1,0:T(8,128)(2,1)S(1)} %get-tuple-element.275), channel_id=1, source_target_pairs={{0,2},{2,0},{4,6},{6,4},{8,10},{10,8},{12,14},{14,12},{16,18},{18,... | collective-permute-start | bytes 2359304 | tf_op jit(solution)/shard_map/ppermute | solution.py:25
  9.9 37.3 %collective-permute-start.7 = (bf16[1536,768]{1,0:T(8,128)(2,1)}, bf16[1536,768]{1,0:T(8,128)(2,1)}, u32[]{:S(2)}, u32[]{:S(2)}) collective-permute-start(bf16[1536,768]{1,0:T(8,128)(2,1)} %wd_ref.3), channel_id=1, source_target_pairs={{0,1},{1,0},{2,3},{3,2},{4,5},{5,4},{6,7},{7,6},{8,9},{9,8},{10,11... | collective-permute-start | bytes 7077896 | tf_op jit(solution)/shard_map/ppermute | solution.py:25
  10.0 37.3 %collective-permute-start.5 = (bf16[768,1536]{1,0:T(8,128)(2,1)}, bf16[768,1536]{1,0:T(8,128)(2,1)}, u32[]{:S(2)}, u32[]{:S(2)}) collective-permute-start(bf16[768,1536]{1,0:T(8,128)(2,1)} %wi_ref.3), channel_id=1, source_target_pairs={{0,1},{1,0},{2,3},{3,2},{4,5},{5,4},{6,7},{7,6},{8,9},{9,8},{10,11... | collective-permute-start | bytes 7077896 | tf_op jit(solution)/shard_map/ppermute | solution.py:25
  23.1 24.2 %collective-permute-start.6 = (f32[1,1536]{1,0:T(1,128)S(1)}, f32[1,1536]{1,0:T(1,128)S(1)}, u32[]{:S(2)}, u32[]{:S(2)}) collective-permute-start(f32[1,1536]{1,0:T(1,128)S(1)} %broadcast_in_dim.10.bi_ref), channel_id=1, source_target_pairs={{0,1},{1,0},{2,3},{3,2},{4,5},{5,4},{6,7},{7,6},{8,9},{9,8},{10,11... | collective-permute-start | bytes 18440 | tf_op jit(solution)/shard_map/ppermute | solution.py:25
  23.7 23.6 %collective-permute-start.8 = (bf16[512,768]{1,0:T(8,128)(2,1)}, bf16[512,768]{1,0:T(8,128)(2,1)S(1)}, u32[]{:S(2)}, u32[]{:S(2)}) collective-permute-start(bf16[512,768]{1,0:T(8,128)(2,1)} %get-tuple-element.143), channel_id=1, source_target_pairs={{0,2},{2,0},{4,6},{6,4},{8,10},{10,8},{12,14},{14,12},{16,18},{18,... | collective-permute-start | bytes 2359304 | tf_op jit(solution)/shard_map/ppermute | solution.py:25
  82.4 15.4 %collective-permute-start.10 = (bf16[8,48,768]{2,1,0:T(8,128)(2,1)S(1)}, bf16[8,48,768]{2,1,0:T(8,128)(2,1)S(1)}, u32[]{:S(2)}, u32[]{:S(2)}) collective-permute-start(bf16[8,48,768]{2,1,0:T(8,128)(2,1)S(1)} %get-tuple-element.150), channel_id=1, source_target_pairs={{0,2},{2,0},{4,6},{6,4},{8,10},{10,8},{12,14},{14,12},{16,18},{18,... | collective-permute-start | bytes 1769480 | tf_op jit(solution)/shard_map/ppermute | solution.py:25
  84.0 15.1 %collective-permute-start.11 = (bf16[8,48,768]{2,1,0:T(8,128)(2,1)S(1)}, bf16[8,48,768]{2,1,0:T(8,128)(2,1)S(1)}, u32[]{:S(2)}, u32[]{:S(2)}) collective-permute-start(bf16[8,48,768]{2,1,0:T(8,128)(2,1)S(1)} %get-tuple-element.151), channel_id=1, source_target_pairs={{0,4},{2,6},{4,0},{6,2},{8,12},{10,14},{12,8},{14,10},{16,20},{18,... | collective-permute-start | bytes 1769480 | tf_op jit(solution)/shard_map/ppermute | solution.py:25
  99.3 21.2 %collective-permute-start.13 = (bf16[2,768,768]{2,1,0:T(8,128)(2,1)S(1)}, bf16[2,768,768]{2,1,0:T(8,128)(2,1)S(1)}, u32[]{:S(2)}, u32[]{:S(2)}) collective-permute-start(bf16[2,768,768]{2,1,0:T(8,128)(2,1)S(1)} %get-tuple-element.171), channel_id=1, source_target_pairs={{0,1},{1,0},{2,3},{3,2},{4,5},{5,4},{6,7},{7,6},{8,9},{9,8},{10,11... | collective-permute-start | bytes 7077896 | tf_op jit(solution)/shard_map/ppermute | solution.py:25
  99.4 19.1 %collective-permute-start.14 = (bf16[4,48,768]{2,1,0:T(8,128)(2,1)S(1)}, bf16[4,48,768]{2,1,0:T(8,128)(2,1)S(1)}, u32[]{:S(2)}, u32[]{:S(2)}) collective-permute-start(bf16[4,48,768]{2,1,0:T(8,128)(2,1)S(1)} %get-tuple-element.160), channel_id=1, source_target_pairs={{0,4},{2,6},{4,0},{6,2},{8,12},{10,14},{12,8},{14,10},{16,20},{18,... | collective-permute-start | bytes 884744 | tf_op jit(solution)/shard_map/ppermute | solution.py:25
  101.0 17.5 %collective-permute-start.15 = (bf16[4,48,768]{2,1,0:T(8,128)(2,1)S(1)}, bf16[4,48,768]{2,1,0:T(8,128)(2,1)S(1)}, u32[]{:S(2)}, u32[]{:S(2)}) collective-permute-start(bf16[4,48,768]{2,1,0:T(8,128)(2,1)S(1)} %get-tuple-element.161), channel_id=1, source_target_pairs={{0,2},{2,0},{4,6},{6,4},{8,10},{10,8},{12,14},{14,12},{16,18},{18,... | collective-permute-start | bytes 884744 | tf_op jit(solution)/shard_map/ppermute | solution.py:25
  101.5 17.0 %collective-permute-start.12 = (bf16[256,768]{1,0:T(8,128)(2,1)S(1)}, bf16[256,768]{1,0:T(8,128)(2,1)S(1)}, u32[]{:S(2)}, u32[]{:S(2)}) collective-permute-start(bf16[256,768]{1,0:T(8,128)(2,1)S(1)} %get-tuple-element.162), channel_id=1, source_target_pairs={{0,2},{2,0},{4,6},{6,4},{8,10},{10,8},{12,14},{14,12},{16,18},{18,... | collective-permute-start | bytes 1179656 | tf_op jit(solution)/shard_map/ppermute | solution.py:25
  121.4 27.3 %collective-permute-start.20 = (bf16[2,96,768]{2,1,0:T(8,128)(2,1)S(1)}, bf16[2,96,768]{2,1,0:T(8,128)(2,1)S(1)}, u32[]{:S(2)}, u32[]{:S(2)}) collective-permute-start(bf16[2,96,768]{2,1,0:T(8,128)(2,1)S(1)} %get-tuple-element.178), channel_id=1, source_target_pairs={{0,8},{2,10},{4,12},{6,14},{8,0},{10,2},{12,4},{14,6},{16,24},{18,... | collective-permute-start | bytes 884744 | tf_op jit(solution)/shard_map/ppermute | solution.py:25
  123.0 25.6 %collective-permute-start.18 = (bf16[8,56,768]{2,1,0:T(8,128)(2,1)S(1)}, bf16[8,56,768]{2,1,0:T(8,128)(2,1)S(1)}, u32[]{:S(2)}, u32[]{:S(2)}) collective-permute-start(bf16[8,56,768]{2,1,0:T(8,128)(2,1)S(1)} %get-tuple-element.176), channel_id=1, source_target_pairs={{0,2},{2,0},{4,6},{6,4},{8,10},{10,8},{12,14},{14,12},{16,18},{18,... | collective-permute-start | bytes 2064392 | tf_op jit(solution)/shard_map/ppermute | solution.py:25
  123.6 25.1 %collective-permute-start.19 = (bf16[8,64,768]{2,1,0:T(8,128)(2,1)S(1)}, bf16[8,64,768]{2,1,0:T(8,128)(2,1)S(1)}, u32[]{:S(2)}, u32[]{:S(2)}) collective-permute-start(bf16[8,64,768]{2,1,0:T(8,128)(2,1)S(1)} %get-tuple-element.177), channel_id=1, source_target_pairs={{0,4},{2,6},{4,0},{6,2},{8,12},{10,14},{12,8},{14,10},{16,20},{18,... | collective-permute-start | bytes 2359304 | tf_op jit(solution)/shard_map/ppermute | solution.py:25
  124.1 24.6 %collective-permute-start.17 = (bf16[256,768]{1,0:T(8,128)(2,1)S(1)}, bf16[256,768]{1,0:T(8,128)(2,1)S(1)}, u32[]{:S(2)}, u32[]{:S(2)}) collective-permute-start(bf16[256,768]{1,0:T(8,128)(2,1)S(1)} %get-tuple-element.179), channel_id=1, source_target_pairs={{0,2},{2,0},{4,6},{6,4},{8,10},{10,8},{12,14},{14,12},{16,18},{18,... | collective-permute-start | bytes 1179656 | tf_op jit(solution)/shard_map/ppermute | solution.py:25
  163.9 16.6 %collective-permute-start.26 = (bf16[8,80,384]{2,1,0:T(8,128)(2,1)S(1)}, bf16[8,80,384]{2,1,0:T(8,128)(2,1)S(1)}, u32[]{:S(2)}, u32[]{:S(2)}) collective-permute-start(bf16[8,80,384]{2,1,0:T(8,128)(2,1)S(1)} %get-tuple-element.205), channel_id=1, source_target_pairs={{0,2},{2,0},{4,6},{6,4},{8,10},{10,8},{12,14},{14,12},{16,18},{18,... | collective-permute-start | bytes 1474568 | tf_op jit(solution)/shard_map/ppermute | solution.py:25
  165.4 15.1 %collective-permute-start.27 = (bf16[8,64,384]{2,1,0:T(8,128)(2,1)S(1)}, bf16[8,64,384]{2,1,0:T(8,128)(2,1)S(1)}, u32[]{:S(2)}, u32[]{:S(2)}) collective-permute-start(bf16[8,64,384]{2,1,0:T(8,128)(2,1)S(1)} %get-tuple-element.206), channel_id=1, source_target_pairs={{0,4},{2,6},{4,0},{6,2},{8,12},{10,14},{12,8},{14,10},{16,20},{18,... | collective-permute-start | bytes 1179656 | tf_op jit(solution)/shard_map/ppermute | solution.py:25
  182.4 16.9 %collective-permute-start.33 = (bf16[1,120,768]{2,1,0:T(8,128)(2,1)}, bf16[1,120,768]{2,1,0:T(8,128)(2,1)S(1)}, u32[]{:S(2)}, u32[]{:S(2)}) collective-permute-start(bf16[1,120,768]{2,1,0:T(8,128)(2,1)} %copy-done.5), channel_id=1, source_target_pairs={{0,16},{2,18},{4,20},{6,22},{8,24},{10,26},{12,28},{14,30},{16,0},... | collective-permute-start | bytes 552968 | tf_op jit(solution)/shard_map/ppermute | solution.py:25
  183.9 15.5 %collective-permute-start.32 = (bf16[4,64,384]{2,1,0:T(8,128)(2,1)S(1)}, bf16[4,64,384]{2,1,0:T(8,128)(2,1)S(1)}, u32[]{:S(2)}, u32[]{:S(2)}) collective-permute-start(bf16[4,64,384]{2,1,0:T(8,128)(2,1)S(1)} %get-tuple-element.222), channel_id=1, source_target_pairs={{0,2},{2,0},{4,6},{6,4},{8,10},{10,8},{12,14},{14,12},{16,18},{18,... | collective-permute-start | bytes 589832 | tf_op jit(solution)/shard_map/ppermute | solution.py:25
  201.4 15.7 %collective-permute-start.40 = (bf16[4,48,768]{2,1,0:T(8,128)(2,1)S(1)}, bf16[4,48,768]{2,1,0:T(8,128)(2,1)S(1)}, u32[]{:S(2)}, u32[]{:S(2)}) collective-permute-start(bf16[4,48,768]{2,1,0:T(8,128)(2,1)S(1)} %get-tuple-element.240.refs_5_), channel_id=1, source_target_pairs={{0,2},{2,0},{4,6},{6,4},{8,10},{10,8},{12,14},{14,12},{16,18},{18,... | collective-permute-start | bytes 884744 | tf_op jit(solution)/shard_map/ppermute | solution.py:25
  241.5 21.9 %collective-permute-start.50 = (bf16[8,72,768]{2,1,0:T(8,128)(2,1)S(1)}, bf16[8,72,768]{2,1,0:T(8,128)(2,1)S(1)}, u32[]{:S(2)}, u32[]{:S(2)}) collective-permute-start(bf16[8,72,768]{2,1,0:T(8,128)(2,1)S(1)} %get-tuple-element.256.refs_1_), channel_id=1, source_target_pairs={{0,4},{2,6},{4,0},{6,2},{8,12},{10,14},{12,8},{14,10},{16,20},{18,... | collective-permute-start | bytes 2654216 | tf_op jit(solution)/shard_map/ppermute | solution.py:25
  242.0 19.3 %collective-permute-start.49 = (bf16[8,64,768]{2,1,0:T(8,128)(2,1)}, bf16[8,64,768]{2,1,0:T(8,128)(2,1)}, u32[]{:S(2)}, u32[]{:S(2)}) collective-permute-start(bf16[8,64,768]{2,1,0:T(8,128)(2,1)} %get-tuple-element.255.refs_0_), channel_id=1, source_target_pairs={{0,2},{2,0},{4,6},{6,4},{8,10},{10,8},{12,14},{14,12},{16,18},{18,... | collective-permute-start | bytes 2359304 | tf_op jit(solution)/shard_map/ppermute | solution.py:25
  249.5 18.5 %collective-permute-start.51 = (bf16[4,80,384]{2,1,0:T(8,128)(2,1)}, bf16[4,80,384]{2,1,0:T(8,128)(2,1)}, u32[]{:S(2)}, u32[]{:S(2)}) collective-permute-start(bf16[4,80,384]{2,1,0:T(8,128)(2,1)} %get-tuple-element.252.refs_0_), channel_id=1, source_target_pairs={{0,4},{2,6},{4,0},{6,2},{8,12},{10,14},{12,8},{14,10},{16,20},{18,... | collective-permute-start | bytes 737288 | tf_op jit(solution)/shard_map/ppermute | solution.py:25
  251.0 16.9 %collective-permute-start.52 = (bf16[4,64,384]{2,1,0:T(8,128)(2,1)}, bf16[4,64,384]{2,1,0:T(8,128)(2,1)}, u32[]{:S(2)}, u32[]{:S(2)}) collective-permute-start(bf16[4,64,384]{2,1,0:T(8,128)(2,1)} %get-tuple-element.253.refs_1_), channel_id=1, source_target_pairs={{0,2},{2,0},{4,6},{6,4},{8,10},{10,8},{12,14},{14,12},{16,18},{18,... | collective-permute-start | bytes 589832 | tf_op jit(solution)/shard_map/ppermute | solution.py:25
  (55 other events, 484.4 us)

commit v2 on v1

--- a/solution.py
+++ b/solution.py
@@ -475,7 +475,7 @@
         i, n, q_n, d_n = unit
         return dot(blocks[i][2], q_n, NT), dot(blocks[i][3], d_n, NT)
 
-    ahead = 1
+    ahead = 2
     ready = [products(unit) for unit in units[:ahead]]
     found = []
     for at, (i, n, q_n, d_n) in enumerate(units):

time: 287 us -> 287 us (level)
  no operation moved by 1% of the time
where the time goes in v2:
time: 287 us; the launch traced here: 282 us
  Pallas kernels  135 us (47%)
  waiting for transfers between devices  85.8 us (30%)
  starting transfers between devices  45.6 us (16%)
  local copies, waits for them, and re-layouts  8.64 us (3%)
  other arithmetic  5.1 us (2%)
    ppermute x55, waiting for transfers between devices, swap_bit(): lax.ppermute(x, axis, [(i, i ^ 1 << bit) for i in range(lax.axis_size(axi...  85.8 us
    ppermute x55, starting transfers between devices, swap_bit(): lax.ppermute(x, axis, [(i, i ^ 1 << bit) for i in range(lax.axis_size(axi...  45.6 us
    pallas_call x2, Pallas kernels, attention_back(): pl.pallas_call(functools.partial(attend_back_kernel, ends), grid=(pairs,)...  30.1 us
    pallas_call x1, Pallas kernels, ffn(): pl.pallas_call(functools.partial(ffn_kernel, tiles), grid=(tiles + per,),...  29.9 us
    pallas_call x2, Pallas kernels, ffn_back(): pl.pallas_call(functools.partial(ffn_back_kernel, last), grid=(tiles,), i...  25.9 us
    pallas_call x1, Pallas kernels, attention(): pl.pallas_call(functools.partial(attend_kernel, pairs), grid=(pairs,), in...  21.8 us
    pallas_call x15, Pallas kernels, advance(): pl.pallas_call(kernel, in_specs=[pl.BlockSpec(memory_space=pltpu.SMEM)] +...  15.6 us
    pallas_call x1, Pallas kernels, input_gradient(): pl.pallas_call(input_kernel, grid=(pairs,), in_specs=[pl.BlockSpec(part,...  8.82 us
  transfers between devices with their start and end apart: 55, of which 23 were waited for; matrix products, arithmetic and copies ran while one was open for 4% of the time, Pallas kernels for 35%

profile of v2, /device:TPU:0, one launch (start us, length us, event | category | flops | bytes accessed | tf_op | source)
XLA Modules:
  0.0 281.8 jit_solution(14797168028656432417)
XLA Ops:
  2.3 3.0 %collective-permute-start = (bf16[512,768]{1,0:T(8,128)(2,1)S(1)}, bf16[512,768]{1,0:T(8,128)(2,1)S(1)}, u32[]{:S(2)}, u32[]{:S(2)}) collective-permute-start(bf16[512,768]{1,0:T(8,128)(2,1)S(1)} %get-tuple-element.275), channel_id=1, source_target_pairs={{0,2},{2,0},{4,6},{6,4},{8,10},{10,8},{12,14},{14,12},{16,18},{18,... | collective-permute-start | bytes 2359304 | tf_op jit(solution)/shard_map/ppermute | solution.py:25
  7.1 2.4 constant_dynamic-slice_fusion
  11.0 5.4 %collective-permute-done.1.mq_ref = bf16[768,384]{1,0:T(8,128)(2,1)S(1)} collective-permute-done((bf16[768,384]{1,0:T(8,128)(2,1)}, bf16[768,384]{1,0:T(8,128)(2,1)S(1)}, u32[]{:S(2)}, u32[]{:S(2)}) %collective-permute-start.1) | collective-permute-done | bytes 589856 | tf_op jit(solution)/shard_map/ppermute | solution.py:25
  16.6 6.2 %collective-permute-done.xb_ref = bf16[512,768]{1,0:T(8,128)(2,1)S(1)} collective-permute-done((bf16[512,768]{1,0:T(8,128)(2,1)S(1)}, bf16[512,768]{1,0:T(8,128)(2,1)S(1)}, u32[]{:S(2)}, u32[]{:S(2)}) %collective-permute-start) | collective-permute-done | bytes 786464 | tf_op jit(solution)/shard_map/ppermute | solution.py:25
  25.4 21.8 %attention_forward.1 = (bf16[1024,2304]{1,0:T(8,128)(2,1)}, f32[6,2,1024]{2,1,0:T(2,128)S(1)}, bf16[768,1024]{1,0:T(8,128)(2,1)}, bf16[768,1024]{1,0:T(8,128)(2,...) custom-call(s32[1,768]{1,0:T(1,128)S(1)} %broadcast_in_dim_reshape.3.swap_ref, ...), custom_call_target="tpu_custom_call" | custom-call | flops 11274289152 | bytes 18874368 | tf_op jit(solution)/shard_map/attention_forward/pallas_call | solution.py:154
  47.3 29.9 %feed_forward.1 = (bf16[1536,1024]{1,0:T(8,128)(2,1)S(1)}, bf16[1024,3072]{1,0:T(8,128)(2,1)}, bf16[768,1024]{1,0:T(8,128)(2,1)S(1)}, bf16[512,768]{1,0:T(8,128)...) custom-call(f32[1024,768]{1,0:T(8,128)} %get-tuple-element.141.mid_n, ...), custom_call_target="tpu_custom_call" | custom-call | flops 9663676416 | bytes 34603008 | tf_op jit(solution)/shard_map/feed_forward/pallas_call | solution.py:270
  77.3 3.0 %weight_gradient.1 = bf16[1536,768]{1,0:T(8,128)(2,1)S(1)} custom-call(bf16[1536,1024]{1,0:T(8,128)(2,1)S(1)} %get-tuple-element.147.a_ref, bf16[1024,768]{1,0:T(8,128)(2,1)S(1)} %get-tuple-element.164.b_ref.df_ref), custom_call_target="tpu_custom_call" | custom-call | flops 2415919104 | bytes 7077888 | tf_op jit(solution)/shard_map/weight_gradient/pallas_call | solution.py:333
  85.5 10.4 %feed_forward_back.2 = (bf16[2,768,768]{2,1,0:T(8,128)(2,1)S(1)}, f32[1,1536]{1,0:T(1,128)S(1)}, f32[1024,768]{1,0:T(8,128)S(1)}) custom-call(bf16[1024,768]{1,0:T(8,128)(2,1)S(1)} %get-tuple-element.164.b_ref.df_ref, bf16[1024,3072]{1,0:T(8,128)(2,1)} %get-tuple-element.153.slope_ref, bf16[768,1536]{1,0:T(8,128)(2,1)} %collective-permute-done.5.mi_ref.wi_ref, ...), custom_call_target="tpu_custom_call" | custom-call | flops 7247757312 | bytes 24379392 | tf_op jit(solution)/shard_map/feed_forward_back/pallas_call | solution.py:422
  103.0 15.4 %feed_forward_back.3 = (bf16[2,768,768]{2,1,0:T(8,128)(2,1)S(1)}, f32[1,1536]{1,0:T(1,128)S(1)}, bf16[384,768]{1,0:T(8,128)(2,1)S(1)}, bf16[384,768]{1,0:T(8,128...) custom-call(bf16[1024,768]{1,0:T(8,128)(2,1)S(1)} %get-tuple-element.164.b_ref.df_ref, ...), custom_call_target="tpu_custom_call" | custom-call | flops 7247757312 | bytes 24379392 | tf_op jit(solution)/shard_map/feed_forward_back/pallas_call | solution.py:422
  125.6 19.8 %attention_backward.2 = (bf16[1,768,384]{2,1,0:T(8,128)(2,1)S(1)}, bf16[2,768,384]{2,1,0:T(8,128)(2,1)S(1)}, bf16[1,768,384]{2,1,0:T(8,128)(2,1)S(1)}, bf16[1024,1536]{1,0:T(8,128)(2,1)}) custom-call(s32[1,768]{1,0:T(1,128)S(1)} %broadcast_in_dim_reshape.3.swap_ref, bf16[1024,2304]{1,0:T(8,128)(2,1)} %get-tuple-element.180.qkv_ref, ...), custom_call_target="tpu_custom_call" | custom-call | flops 13958643712 | bytes 11010048 | tf_op jit(solution)/shard_map/attention_backward/pallas_call | solution.py:533
  145.4 3.2 %collective-permute-done.17 = bf16[256,768]{1,0:T(8,128)(2,1)S(1)} collective-permute-done((bf16[256,768]{1,0:T(8,128)(2,1)S(1)}, bf16[256,768]{1,0:T(8,128)(2,1)S(1)}, u32[]{:S(2)}, u32[]{:S(2)}) %collective-permute-start.17) | collective-permute-done | bytes 393248 | tf_op jit(solution)/shard_map/ppermute | solution.py:25
  149.2 2.7 collective-permute-start.25
  152.9 10.3 %attention_backward.3 = (bf16[2,768,384]{2,1,0:T(8,128)(2,1)S(1)}, bf16[1024,768]{1,0:T(8,128)(2,1)}) custom-call(s32[1,768]{1,0:T(1,128)S(1)} %broadcast_in_dim_reshape.3.swap_ref, bf16[1024,2304]{1,0:T(8,128)(2,1)} %get-tuple-element.180.qkv_ref, bf16[768,1024]{1,0:T(8,128)(2,1)} %get-tuple-element.167.refs_2_.ctx_t_ref, ...), custom_call_target="tpu_custom_call" | custom-call | flops 6979321856 | bytes 11010048 | tf_op jit(solution)/shard_map/attention_backward/pallas_call | solution.py:533
  167.7 8.8 %input_gradient.1 = (f32[512,768]{1,0:T(8,128)S(1)}, bf16[512,768]{1,0:T(8,128)(2,1)S(1)}) custom-call(bf16[1024,1536]{1,0:T(8,128)(2,1)} %get-tuple-element.185.first_ref.mate_ref, bf16[1024,768]{1,0:T(8,128)(2,1)} %get-tuple-element.209.later_ref, bf16[1024,1536]{1,0:T(8,128)(2,1)} %get-tuple-element.185.first_ref.mate_ref, bf16[768,384]{1,0:T(8,128)(2,1)} %wq_ref.3, ...), custom_call_target="tpu_custom_call" | custom-call | flops 3623878656 | bytes 11010048 | tf_op jit(solution)/shard_map/input_gradient/pallas_call | solution.py:586
  186.5 12.8 %collective-permute-done.30 = bf16[256,768]{1,0:T(8,128)(2,1)S(1)} collective-permute-done((bf16[256,768]{1,0:T(8,128)(2,1)S(1)}, bf16[256,768]{1,0:T(8,128)(2,1)S(1)}, u32[]{:S(2)}, u32[]{:S(2)}) %collective-permute-start.30) | collective-permute-done | bytes 393248 | tf_op jit(solution)/shard_map/ppermute | solution.py:25
  204.8 7.6 %collective-permute-done.36 = bf16[256,768]{1,0:T(8,128)(2,1)S(1)} collective-permute-done((bf16[256,768]{1,0:T(8,128)(2,1)S(1)}, bf16[256,768]{1,0:T(8,128)(2,1)S(1)}, u32[]{:S(2)}, u32[]{:S(2)}) %collective-permute-start.36) | collective-permute-done | bytes 393248 | tf_op jit(solution)/shard_map/ppermute | solution.py:25
  213.3 3.8 %collective-permute-done.40.refs_7_ = bf16[4,48,768]{2,1,0:T(8,128)(2,1)S(1)} collective-permute-done((bf16[4,48,768]{2,1,0:T(8,128)(2,1)S(1)}, bf16[4,48,768]{2,1,0:T(8,128)(2,1)S(1)}, u32[]{:S(2)}, u32[]{:S(2)}) %collective-permute-start.40) | collective-permute-done | bytes 294944 | tf_op jit(solution)/shard_map/ppermute | solution.py:25
  220.0 7.5 %collective-permute-done.41.refs_1_ = bf16[1,144,384]{2,1,0:T(8,128)(2,1)S(1)} collective-permute-done((bf16[1,144,384]{2,1,0:T(8,128)(2,1)S(1)}, bf16[1,144,384]{2,1,0:T(8,128)(2,1)S(1)}, u32[]{:S(2)}, u32[]{:S(2)}) %collective-permute-start.41) | collective-permute-done | bytes 110624 | tf_op jit(solution)/shard_map/ppermute | solution.py:25
  232.1 2.5 sum_step.24
  234.6 3.1 %collective-permute-done.45.refs_1_ = bf16[1,144,384]{2,1,0:T(8,128)(2,1)S(1)} collective-permute-done((bf16[1,144,384]{2,1,0:T(8,128)(2,1)S(1)}, bf16[1,144,384]{2,1,0:T(8,128)(2,1)S(1)}, u32[]{:S(2)}, u32[]{:S(2)}) %collective-permute-start.45) | collective-permute-done | bytes 110624 | tf_op jit(solution)/shard_map/ppermute | solution.py:25
  244.4 4.3 %collective-permute-done.48.refs_1_ = bf16[2,144,384]{2,1,0:T(8,128)(2,1)S(1)} collective-permute-done((bf16[2,144,384]{2,1,0:T(8,128)(2,1)S(1)}, bf16[2,144,384]{2,1,0:T(8,128)(2,1)S(1)}, u32[]{:S(2)}, u32[]{:S(2)}) %collective-permute-start.48) | collective-permute-done | bytes 221216 | tf_op jit(solution)/shard_map/ppermute | solution.py:25
  252.4 9.0 %collective-permute-done.49.refs_2_ = bf16[8,64,768]{2,1,0:T(8,128)(2,1)} collective-permute-done((bf16[8,64,768]{2,1,0:T(8,128)(2,1)}, bf16[8,64,768]{2,1,0:T(8,128)(2,1)}, u32[]{:S(2)}, u32[]{:S(2)}) %collective-permute-start.49) | collective-permute-done | bytes 786464 | tf_op jit(solution)/shard_map/ppermute | solution.py:25
  263.5 4.5 %sum_step.27 = (f32[16,48,1536]{2,1,0:T(8,128)}, f32[384,768]{1,0:T(8,128)}, f32[8,768]{1,0:T(8,128)S(1)}) custom-call(s32[1]{0:T(128)} %bitcast.3.place_ref, bf16[8,64,768]{2,1,0:T(8,128)(2,1)} %get-tuple-element.255.refs_0_, bf16[8,72,768]{2,1,0:T(8,128)(2,1)S(1)} %get-tuple-element.256.refs_1_, bf16[8,64,768]{2,1,0:T(8,128)(2,1)} %collective-permute-done.49.refs_2_, ...), custom_call_target="tpu_custom_call" | custom-call | flops 6303744 | bytes 6303744 | tf_op jit(solution)/shard_map/sum_step/pallas_call | solution.py:836
  275.6 4.0 %collective-permute-done.54.refs_3_ = bf16[8,64,384]{2,1,0:T(8,128)(2,1)S(1)} collective-permute-done((bf16[8,64,384]{2,1,0:T(8,128)(2,1)S(1)}, bf16[8,64,384]{2,1,0:T(8,128)(2,1)S(1)}, u32[]{:S(2)}, u32[]{:S(2)}) %collective-permute-start.54) | collective-permute-done | bytes 393248 | tf_op jit(solution)/shard_map/ppermute | solution.py:25
  (198 shorter events, 78.7 us)
Async XLA Ops:
  2.3 20.5 %collective-permute-start = (bf16[512,768]{1,0:T(8,128)(2,1)S(1)}, bf16[512,768]{1,0:T(8,128)(2,1)S(1)}, u32[]{:S(2)}, u32[]{:S(2)}) collective-permute-start(bf16[512,768]{1,0:T(8,128)(2,1)S(1)} %get-tuple-element.275), channel_id=1, source_target_pairs={{0,2},{2,0},{4,6},{6,4},{8,10},{10,8},{12,14},{14,12},{16,18},{18,... | collective-permute-start | bytes 2359304 | tf_op jit(solution)/shard_map/ppermute | solution.py:25
  9.9 37.3 %collective-permute-start.7 = (bf16[1536,768]{1,0:T(8,128)(2,1)}, bf16[1536,768]{1,0:T(8,128)(2,1)}, u32[]{:S(2)}, u32[]{:S(2)}) collective-permute-start(bf16[1536,768]{1,0:T(8,128)(2,1)} %wd_ref.3), channel_id=1, source_target_pairs={{0,1},{1,0},{2,3},{3,2},{4,5},{5,4},{6,7},{7,6},{8,9},{9,8},{10,11... | collective-permute-start | bytes 7077896 | tf_op jit(solution)/shard_map/ppermute | solution.py:25
  10.0 37.3 %collective-permute-start.5 = (bf16[768,1536]{1,0:T(8,128)(2,1)}, bf16[768,1536]{1,0:T(8,128)(2,1)}, u32[]{:S(2)}, u32[]{:S(2)}) collective-permute-start(bf16[768,1536]{1,0:T(8,128)(2,1)} %wi_ref.3), channel_id=1, source_target_pairs={{0,1},{1,0},{2,3},{3,2},{4,5},{5,4},{6,7},{7,6},{8,9},{9,8},{10,11... | collective-permute-start | bytes 7077896 | tf_op jit(solution)/shard_map/ppermute | solution.py:25
  23.1 24.2 %collective-permute-start.6 = (f32[1,1536]{1,0:T(1,128)S(1)}, f32[1,1536]{1,0:T(1,128)S(1)}, u32[]{:S(2)}, u32[]{:S(2)}) collective-permute-start(f32[1,1536]{1,0:T(1,128)S(1)} %broadcast_in_dim.10.bi_ref), channel_id=1, source_target_pairs={{0,1},{1,0},{2,3},{3,2},{4,5},{5,4},{6,7},{7,6},{8,9},{9,8},{10,11... | collective-permute-start | bytes 18440 | tf_op jit(solution)/shard_map/ppermute | solution.py:25
  23.7 23.6 %collective-permute-start.8 = (bf16[512,768]{1,0:T(8,128)(2,1)}, bf16[512,768]{1,0:T(8,128)(2,1)S(1)}, u32[]{:S(2)}, u32[]{:S(2)}) collective-permute-start(bf16[512,768]{1,0:T(8,128)(2,1)} %get-tuple-element.143), channel_id=1, source_target_pairs={{0,2},{2,0},{4,6},{6,4},{8,10},{10,8},{12,14},{14,12},{16,18},{18,... | collective-permute-start | bytes 2359304 | tf_op jit(solution)/shard_map/ppermute | solution.py:25
  82.4 15.4 %collective-permute-start.10 = (bf16[8,48,768]{2,1,0:T(8,128)(2,1)S(1)}, bf16[8,48,768]{2,1,0:T(8,128)(2,1)S(1)}, u32[]{:S(2)}, u32[]{:S(2)}) collective-permute-start(bf16[8,48,768]{2,1,0:T(8,128)(2,1)S(1)} %get-tuple-element.150), channel_id=1, source_target_pairs={{0,2},{2,0},{4,6},{6,4},{8,10},{10,8},{12,14},{14,12},{16,18},{18,... | collective-permute-start | bytes 1769480 | tf_op jit(solution)/shard_map/ppermute | solution.py:25
  84.0 15.1 %collective-permute-start.11 = (bf16[8,48,768]{2,1,0:T(8,128)(2,1)S(1)}, bf16[8,48,768]{2,1,0:T(8,128)(2,1)S(1)}, u32[]{:S(2)}, u32[]{:S(2)}) collective-permute-start(bf16[8,48,768]{2,1,0:T(8,128)(2,1)S(1)} %get-tuple-element.151), channel_id=1, source_target_pairs={{0,4},{2,6},{4,0},{6,2},{8,12},{10,14},{12,8},{14,10},{16,20},{18,... | collective-permute-start | bytes 1769480 | tf_op jit(solution)/shard_map/ppermute | solution.py:25
  99.3 21.2 %collective-permute-start.13 = (bf16[2,768,768]{2,1,0:T(8,128)(2,1)S(1)}, bf16[2,768,768]{2,1,0:T(8,128)(2,1)S(1)}, u32[]{:S(2)}, u32[]{:S(2)}) collective-permute-start(bf16[2,768,768]{2,1,0:T(8,128)(2,1)S(1)} %get-tuple-element.171), channel_id=1, source_target_pairs={{0,1},{1,0},{2,3},{3,2},{4,5},{5,4},{6,7},{7,6},{8,9},{9,8},{10,11... | collective-permute-start | bytes 7077896 | tf_op jit(solution)/shard_map/ppermute | solution.py:25
  99.4 19.1 %collective-permute-start.14 = (bf16[4,48,768]{2,1,0:T(8,128)(2,1)S(1)}, bf16[4,48,768]{2,1,0:T(8,128)(2,1)S(1)}, u32[]{:S(2)}, u32[]{:S(2)}) collective-permute-start(bf16[4,48,768]{2,1,0:T(8,128)(2,1)S(1)} %get-tuple-element.160), channel_id=1, source_target_pairs={{0,4},{2,6},{4,0},{6,2},{8,12},{10,14},{12,8},{14,10},{16,20},{18,... | collective-permute-start | bytes 884744 | tf_op jit(solution)/shard_map/ppermute | solution.py:25
  101.0 17.5 %collective-permute-start.15 = (bf16[4,48,768]{2,1,0:T(8,128)(2,1)S(1)}, bf16[4,48,768]{2,1,0:T(8,128)(2,1)S(1)}, u32[]{:S(2)}, u32[]{:S(2)}) collective-permute-start(bf16[4,48,768]{2,1,0:T(8,128)(2,1)S(1)} %get-tuple-element.161), channel_id=1, source_target_pairs={{0,2},{2,0},{4,6},{6,4},{8,10},{10,8},{12,14},{14,12},{16,18},{18,... | collective-permute-start | bytes 884744 | tf_op jit(solution)/shard_map/ppermute | solution.py:25
  101.5 17.0 %collective-permute-start.12 = (bf16[256,768]{1,0:T(8,128)(2,1)S(1)}, bf16[256,768]{1,0:T(8,128)(2,1)S(1)}, u32[]{:S(2)}, u32[]{:S(2)}) collective-permute-start(bf16[256,768]{1,0:T(8,128)(2,1)S(1)} %get-tuple-element.162), channel_id=1, source_target_pairs={{0,2},{2,0},{4,6},{6,4},{8,10},{10,8},{12,14},{14,12},{16,18},{18,... | collective-permute-start | bytes 1179656 | tf_op jit(solution)/shard_map/ppermute | solution.py:25
  121.4 27.3 %collective-permute-start.20 = (bf16[2,96,768]{2,1,0:T(8,128)(2,1)S(1)}, bf16[2,96,768]{2,1,0:T(8,128)(2,1)S(1)}, u32[]{:S(2)}, u32[]{:S(2)}) collective-permute-start(bf16[2,96,768]{2,1,0:T(8,128)(2,1)S(1)} %get-tuple-element.178), channel_id=1, source_target_pairs={{0,8},{2,10},{4,12},{6,14},{8,0},{10,2},{12,4},{14,6},{16,24},{18,... | collective-permute-start | bytes 884744 | tf_op jit(solution)/shard_map/ppermute | solution.py:25
  123.0 25.6 %collective-permute-start.18 = (bf16[8,56,768]{2,1,0:T(8,128)(2,1)S(1)}, bf16[8,56,768]{2,1,0:T(8,128)(2,1)S(1)}, u32[]{:S(2)}, u32[]{:S(2)}) collective-permute-start(bf16[8,56,768]{2,1,0:T(8,128)(2,1)S(1)} %get-tuple-element.176), channel_id=1, source_target_pairs={{0,2},{2,0},{4,6},{6,4},{8,10},{10,8},{12,14},{14,12},{16,18},{18,... | collective-permute-start | bytes 2064392 | tf_op jit(solution)/shard_map/ppermute | solution.py:25
  123.6 25.1 %collective-permute-start.19 = (bf16[8,64,768]{2,1,0:T(8,128)(2,1)S(1)}, bf16[8,64,768]{2,1,0:T(8,128)(2,1)S(1)}, u32[]{:S(2)}, u32[]{:S(2)}) collective-permute-start(bf16[8,64,768]{2,1,0:T(8,128)(2,1)S(1)} %get-tuple-element.177), channel_id=1, source_target_pairs={{0,4},{2,6},{4,0},{6,2},{8,12},{10,14},{12,8},{14,10},{16,20},{18,... | collective-permute-start | bytes 2359304 | tf_op jit(solution)/shard_map/ppermute | solution.py:25
  124.1 24.6 %collective-permute-start.17 = (bf16[256,768]{1,0:T(8,128)(2,1)S(1)}, bf16[256,768]{1,0:T(8,128)(2,1)S(1)}, u32[]{:S(2)}, u32[]{:S(2)}) collective-permute-start(bf16[256,768]{1,0:T(8,128)(2,1)S(1)} %get-tuple-element.179), channel_id=1, source_target_pairs={{0,2},{2,0},{4,6},{6,4},{8,10},{10,8},{12,14},{14,12},{16,18},{18,... | collective-permute-start | bytes 1179656 | tf_op jit(solution)/shard_map/ppermute | solution.py:25
  163.9 16.6 %collective-permute-start.26 = (bf16[8,80,384]{2,1,0:T(8,128)(2,1)S(1)}, bf16[8,80,384]{2,1,0:T(8,128)(2,1)S(1)}, u32[]{:S(2)}, u32[]{:S(2)}) collective-permute-start(bf16[8,80,384]{2,1,0:T(8,128)(2,1)S(1)} %get-tuple-element.205), channel_id=1, source_target_pairs={{0,2},{2,0},{4,6},{6,4},{8,10},{10,8},{12,14},{14,12},{16,18},{18,... | collective-permute-start | bytes 1474568 | tf_op jit(solution)/shard_map/ppermute | solution.py:25
  165.4 15.1 %collective-permute-start.27 = (bf16[8,64,384]{2,1,0:T(8,128)(2,1)S(1)}, bf16[8,64,384]{2,1,0:T(8,128)(2,1)S(1)}, u32[]{:S(2)}, u32[]{:S(2)}) collective-permute-start(bf16[8,64,384]{2,1,0:T(8,128)(2,1)S(1)} %get-tuple-element.206), channel_id=1, source_target_pairs={{0,4},{2,6},{4,0},{6,2},{8,12},{10,14},{12,8},{14,10},{16,20},{18,... | collective-permute-start | bytes 1179656 | tf_op jit(solution)/shard_map/ppermute | solution.py:25
  182.5 16.9 %collective-permute-start.33 = (bf16[1,120,768]{2,1,0:T(8,128)(2,1)}, bf16[1,120,768]{2,1,0:T(8,128)(2,1)S(1)}, u32[]{:S(2)}, u32[]{:S(2)}) collective-permute-start(bf16[1,120,768]{2,1,0:T(8,128)(2,1)} %copy-done.5), channel_id=1, source_target_pairs={{0,16},{2,18},{4,20},{6,22},{8,24},{10,26},{12,28},{14,30},{16,0},... | collective-permute-start | bytes 552968 | tf_op jit(solution)/shard_map/ppermute | solution.py:25
  183.9 15.5 %collective-permute-start.32 = (bf16[4,64,384]{2,1,0:T(8,128)(2,1)S(1)}, bf16[4,64,384]{2,1,0:T(8,128)(2,1)S(1)}, u32[]{:S(2)}, u32[]{:S(2)}) collective-permute-start(bf16[4,64,384]{2,1,0:T(8,128)(2,1)S(1)} %get-tuple-element.222), channel_id=1, source_target_pairs={{0,2},{2,0},{4,6},{6,4},{8,10},{10,8},{12,14},{14,12},{16,18},{18,... | collective-permute-start | bytes 589832 | tf_op jit(solution)/shard_map/ppermute | solution.py:25
  201.4 15.7 %collective-permute-start.40 = (bf16[4,48,768]{2,1,0:T(8,128)(2,1)S(1)}, bf16[4,48,768]{2,1,0:T(8,128)(2,1)S(1)}, u32[]{:S(2)}, u32[]{:S(2)}) collective-permute-start(bf16[4,48,768]{2,1,0:T(8,128)(2,1)S(1)} %get-tuple-element.240.refs_5_), channel_id=1, source_target_pairs={{0,2},{2,0},{4,6},{6,4},{8,10},{10,8},{12,14},{14,12},{16,18},{18,... | collective-permute-start | bytes 884744 | tf_op jit(solution)/shard_map/ppermute | solution.py:25
  241.6 21.9 %collective-permute-start.50 = (bf16[8,72,768]{2,1,0:T(8,128)(2,1)S(1)}, bf16[8,72,768]{2,1,0:T(8,128)(2,1)S(1)}, u32[]{:S(2)}, u32[]{:S(2)}) collective-permute-start(bf16[8,72,768]{2,1,0:T(8,128)(2,1)S(1)} %get-tuple-element.256.refs_1_), channel_id=1, source_target_pairs={{0,4},{2,6},{4,0},{6,2},{8,12},{10,14},{12,8},{14,10},{16,20},{18,... | collective-permute-start | bytes 2654216 | tf_op jit(solution)/shard_map/ppermute | solution.py:25
  242.1 19.3 %collective-permute-start.49 = (bf16[8,64,768]{2,1,0:T(8,128)(2,1)}, bf16[8,64,768]{2,1,0:T(8,128)(2,1)}, u32[]{:S(2)}, u32[]{:S(2)}) collective-permute-start(bf16[8,64,768]{2,1,0:T(8,128)(2,1)} %get-tuple-element.255.refs_0_), channel_id=1, source_target_pairs={{0,2},{2,0},{4,6},{6,4},{8,10},{10,8},{12,14},{14,12},{16,18},{18,... | collective-permute-start | bytes 2359304 | tf_op jit(solution)/shard_map/ppermute | solution.py:25
  249.5 18.5 %collective-permute-start.51 = (bf16[4,80,384]{2,1,0:T(8,128)(2,1)}, bf16[4,80,384]{2,1,0:T(8,128)(2,1)}, u32[]{:S(2)}, u32[]{:S(2)}) collective-permute-start(bf16[4,80,384]{2,1,0:T(8,128)(2,1)} %get-tuple-element.252.refs_0_), channel_id=1, source_target_pairs={{0,4},{2,6},{4,0},{6,2},{8,12},{10,14},{12,8},{14,10},{16,20},{18,... | collective-permute-start | bytes 737288 | tf_op jit(solution)/shard_map/ppermute | solution.py:25
  251.0 16.9 %collective-permute-start.52 = (bf16[4,64,384]{2,1,0:T(8,128)(2,1)}, bf16[4,64,384]{2,1,0:T(8,128)(2,1)}, u32[]{:S(2)}, u32[]{:S(2)}) collective-permute-start(bf16[4,64,384]{2,1,0:T(8,128)(2,1)} %get-tuple-element.253.refs_1_), channel_id=1, source_target_pairs={{0,2},{2,0},{4,6},{6,4},{8,10},{10,8},{12,14},{14,12},{16,18},{18,... | collective-permute-start | bytes 589832 | tf_op jit(solution)/shard_map/ppermute | solution.py:25
  (55 other events, 484.5 us)
